TPU v7x, 32 devices: a whole 2x2x4 slice. The times are simulated.
32 devices in a mesh: ray: 8 (over y, x, core), tile: 4 (over z).
Axes of the slice: x: 2, y: 2, z: 4, core: 2. Of those that a mesh axis runs over, the one named last changes fastest.
Arguments:
- volume: bfloat16 [32, 16, 16, 256], P('tile'), may hold values from -8 to 8
- sample_cells: int32 [512, 128], P(('ray', 'tile')), may hold values from 0 to 8191, as said below
- sample_fracs: float32 [3, 512, 128], P(None, ('ray', 'tile')), may hold values from 0 to 1
- view_mask: int32 [512, 128], P(('ray', 'tile')), may hold values 0 or 1
- pixel_of_ray: int32 [32, 16], P(('ray', 'tile')), may hold values from 0 to 15, each once within a row
- conv_weight: bfloat16 [2, 27, 256, 256], replicated, may hold values from -0.078125 to 0.078125
- norm_gain: float32 [2, 256], replicated, may hold values from 0.5 to 1.5
- norm_shift: float32 [2, 256], replicated, may hold values from -3 to 3
- hidden_weight: bfloat16 [2, 256, 256], replicated, may hold values from -0.375 to 0.375
- hidden_bias: float32 [2, 256], replicated, may hold values from -3 to 3
- density_weight: bfloat16 [2, 256], replicated, may hold values from -0.375 to 0.375
- density_bias: float32 [2], replicated, may hold values from -2 to 2
- semantic_weight: bfloat16 [2, 256, 18], replicated, may hold values from -0.375 to 0.375
- semantic_bias: float32 [2, 18], replicated, may hold values from -4 to 4
- render_cotangent: bfloat16 [2, 512, 19], P(None, ('ray', 'tile')), may hold values from -6 to 6
- volume_cotangent: bfloat16 [32, 16, 16, 256], P('tile'), may hold values from -6 to 6
Outputs:
- rendered: float32 [2, 512, 19], P(None, ('ray', 'tile'))
- volume_out: bfloat16 [32, 16, 16, 256], P('tile')
- volume_grad: float32 [32, 16, 16, 256], P('tile')
- conv_grad: float32 [2, 27, 256, 256], replicated
- gain_grad: float32 [2, 256], replicated
- shift_grad: float32 [2, 256], replicated
- hidden_weight_grad: float32 [2, 256, 256], replicated
- hidden_bias_grad: float32 [2, 256], replicated
- density_weight_grad: float32 [2, 256], replicated
- density_bias_grad: float32 [2], replicated
- semantic_weight_grad: float32 [2, 256, 18], replicated
- semantic_bias_grad: float32 [2, 18], replicated
Inputs may be any that keep to these rules, and one draw needn't show every extreme that they name: `sample_cells`: on the rays of one device exactly 768 samples lie in one tile of 8 x-planes, the same tile for all devices with the same index along ray; the remaining samples are spread over the other tiles as evenly as their number allows. A sample's cell is never on the last plane of its tile along x, nor on the last plane along y or z.
All inputs are finite; a program needn't handle non-finite values. No bound on the sum of `view_mask` on one device may be relied on, other than what follows from the above.
Results may differ from a plain program's by a relative error of at most 0.0052.
Values may be sent and summed in bfloat16 or wider, within the bound.
No kernel may reach another device: no remote copies, remote signals or barrier semaphores. Data moves between devices by JAX's collectives and lax.ppermute only.
A program may use at most 256 MiB of HBM per device.

v0:
```python
import jax
import jax.numpy as jnp
from jax import lax
from jax.sharding import PartitionSpec as P

CAP = 768


epsilon = 1e-05


def padded_2(shard, sides, width):
    for axis, dim in sides:
        devices, length = (lax.axis_size(axis), shard.shape[dim])
        up = [(i, (i + 1) % devices) for i in range(devices - 1)]
        down = [(j, i) for i, j in up]
        last = lax.slice_in_dim(shard, length - width, length, axis=dim)
        leading = lax.slice_in_dim(shard, 0, width, axis=dim)
        before = lax.ppermute(last, axis, up)
        after = lax.ppermute(leading, axis, down)
        shard = jnp.concatenate([before, shard, after], axis=dim)
    return shard


def offsets():
    return [(a, b, c) for a in range(3) for b in range(3) for c in range(3)]


def shifted(padded, a, b, c, shape):
    depth, height, width, channels = shape
    return padded[a : a + depth, b : b + height, c : c + width].reshape(
        depth * height * width, channels
    )


def pad_inner(values):
    return jnp.pad(values, ((0, 0), (1, 1), (1, 1), (0, 0)))


def convolve_rows(padded, weight, shape, count):
    total = jnp.zeros((count, weight.shape[2]), jnp.float32)
    for number, (a, b, c) in enumerate(offsets()):
        piece = shifted(padded, a, b, c, shape)
        total = total + jnp.dot(piece, weight[number], preferred_element_type=jnp.float32)
    return total


def convolve_back_rows(padded, weight, shape, count):
    total = jnp.zeros((count, weight.shape[1]), jnp.float32)
    for number, (a, b, c) in enumerate(offsets()):
        piece = shifted(padded, 2 - a, 2 - b, 2 - c, shape)
        total = total + lax.dot_general(
            piece, weight[number], (((1,), (1,)), ((), ())), preferred_element_type=jnp.float32
        )
    return total


def weight_terms(padded, grad_rows, start, shape):
    terms = []
    for a, b, c in offsets():
        piece = lax.dynamic_slice_in_dim(
            shifted(padded, a, b, c, shape), start, grad_rows.shape[0], 0
        )
        terms.append(
            lax.dot_general(
                piece, grad_rows, (((0,), (0,)), ((), ())), preferred_element_type=jnp.float32
            )
        )
    return jnp.stack(terms)


def axis_weights(base, frac, size):
    grid = jnp.arange(size, dtype=jnp.float32)[None, :]
    lower = jnp.where(grid == base[:, None], 1.0 - frac[:, None], 0.0)
    upper = jnp.where(grid == base[:, None] + 1.0, frac[:, None], 0.0)
    return lower + upper


def trilinear(coords, shape):
    along_x = axis_weights(coords[0], coords[3], shape[0])
    along_y = axis_weights(coords[1], coords[4], shape[1])
    along_z = axis_weights(coords[2], coords[5], shape[2])
    table = along_x[:, :, None, None] * along_y[:, None, :, None] * along_z[:, None, None, :]
    return table.reshape(coords.shape[1], shape[0] * shape[1] * shape[2]).astype(jnp.bfloat16)


def per_device(
    volume,
    sample_cells,
    sample_fracs,
    view_mask,
    pixel_of_ray,
    conv_weight,
    norm_gain,
    norm_shift,
    hidden_weight,
    hidden_bias,
    density_weight,
    density_bias,
    semantic_weight,
    semantic_bias,
    render_cotangent,
    volume_cotangent,
):
    shape = volume.shape
    depth, height, width, channels = shape
    voxels = depth * height * width
    tiles = lax.axis_size("tile")
    every_voxel = float(voxels * tiles)
    rays, samples = sample_cells.shape
    count = rays * samples
    classes = semantic_weight.shape[2]
    layers = conv_weight.shape[0]
    capacity = CAP
    step = 4.0 / samples
    cells = sample_cells.reshape(count)
    owner = cells // voxels
    local = cells % voxels
    base_x = local // (height * width)
    base_y = local // width % height
    base_z = local % width
    chosen = (owner[:, None] == jnp.arange(tiles, dtype=jnp.int32)[None, :]).astype(jnp.int32)
    slot = jnp.sum((jnp.cumsum(chosen, axis=0) - 1) * chosen, axis=1)
    target = owner * capacity + slot
    values = jnp.concatenate(
        [jnp.stack([base_x, base_y, base_z]).astype(jnp.float32), sample_fracs.reshape(3, count)],
        axis=0,
    )
    empty = jnp.concatenate(
        [
            jnp.full((3, tiles * capacity), -10.0, jnp.float32),
            jnp.zeros((3, tiles * capacity), jnp.float32),
        ],
        axis=0,
    )
    buffer = empty.at[:, target].set(values).reshape(6, tiles, capacity)
    received = lax.all_to_all(buffer, "tile", split_axis=1, concat_axis=1, tiled=True)
    visible = view_mask.astype(jnp.float32)
    pixels = pixel_of_ray[0]
    current_rows = volume.reshape(voxels, channels).astype(jnp.float32)
    rounded = volume
    kept = []
    pictures = []
    for layer in range(layers):
        padded = pad_inner(padded_2(rounded, (("tile", 0),), 1))
        conv_out = convolve_rows(padded, conv_weight[layer], shape, voxels)
        partial_stats = (jnp.sum(conv_out, axis=0), jnp.sum(conv_out * conv_out, axis=0))
        totals, squares = lax.psum((partial_stats[0], partial_stats[1]), "tile")
        mean = totals / every_voxel
        inverse = lax.rsqrt(squares / every_voxel - mean * mean + epsilon)
        normal = (conv_out - mean) * inverse * norm_gain[layer] + norm_shift[layer]
        current_rows = current_rows + jax.nn.silu(normal)
        rounded_rows = current_rows.astype(jnp.bfloat16)
        rounded = rounded_rows.reshape(shape)
        pieces = [
            jnp.dot(
                trilinear(received[:, source], shape),
                rounded_rows,
                preferred_element_type=jnp.float32,
            ).astype(jnp.bfloat16)
            for source in range(tiles)
        ]
        returned = lax.all_to_all(
            jnp.stack(pieces), "tile", split_axis=0, concat_axis=0, tiled=True
        )
        features = returned.reshape(tiles * capacity, channels)[target]
        inner = (
            jnp.dot(features, hidden_weight[layer], preferred_element_type=jnp.float32)
            + hidden_bias[layer]
        )
        hidden = jax.nn.softplus(inner).astype(jnp.bfloat16)
        head_weight = jnp.concatenate(
            [semantic_weight[layer], density_weight[layer][:, None]], axis=1
        )
        head_bias = jnp.concatenate([semantic_bias[layer], density_bias[layer : layer + 1]])
        heads = jnp.dot(hidden, head_weight, preferred_element_type=jnp.float32) + head_bias
        semantic = heads[:, :classes].reshape(rays, samples, classes)
        density_pre = heads[:, classes].reshape(rays, samples)
        optical = visible * jax.nn.softplus(density_pre) * step
        passing = jnp.exp(-(jnp.cumsum(optical, axis=1) - optical))
        fading = jnp.exp(-optical)
        weights = passing * (1.0 - fading)
        colour = jnp.sum(weights[:, :, None] * semantic, axis=1)
        result = jnp.concatenate([colour, jnp.sum(weights, axis=1)[:, None]], axis=1)
        pictures.append(jnp.zeros_like(result).at[pixels].set(result))
        kept.append(
            (
                padded,
                mean,
                inverse,
                features,
                inner,
                hidden,
                head_weight,
                semantic,
                density_pre,
                passing,
                fading,
                weights,
            )
        )
    conv_grads = [None] * layers
    gain_grads = [None] * layers
    shift_grads = [None] * layers
    hidden_weight_grads = [None] * layers
    hidden_bias_grads = [None] * layers
    head_weight_grads = [None] * layers
    head_bias_grads = [None] * layers
    grad_current = volume_cotangent.reshape(voxels, channels).astype(jnp.float32)
    for layer in reversed(range(layers)):
        (
            padded,
            mean,
            inverse,
            features,
            inner,
            hidden,
            head_weight,
            semantic,
            density_pre,
            passing,
            fading,
            weights,
        ) = kept[layer]
        upstream = render_cotangent[layer].astype(jnp.float32)[pixels]
        grad_semantic = weights[:, :, None] * upstream[:, None, :classes]
        grad_weights = (
            jnp.sum(semantic * upstream[:, None, :classes], axis=2) + upstream[:, classes][:, None]
        )
        carried = grad_weights * weights
        later = jnp.sum(carried, axis=1, keepdims=True) - jnp.cumsum(carried, axis=1)
        grad_optical = grad_weights * passing * fading - later
        grad_density = grad_optical * visible * step * jax.nn.sigmoid(density_pre)
        grad_heads = (
            jnp.concatenate([grad_semantic, grad_density[:, :, None]], axis=2)
            .reshape(count, classes + 1)
            .astype(jnp.bfloat16)
        )
        grad_hidden = lax.dot_general(
            grad_heads, head_weight, (((1,), (1,)), ((), ())), preferred_element_type=jnp.float32
        )
        grad_inner = (grad_hidden * jax.nn.sigmoid(inner)).astype(jnp.bfloat16)
        head_weight_grad = lax.dot_general(
            hidden, grad_heads, (((0,), (0,)), ((), ())), preferred_element_type=jnp.float32
        )
        head_bias_grad = jnp.sum(grad_heads.astype(jnp.float32), axis=0)
        hidden_weight_grad = lax.dot_general(
            features, grad_inner, (((0,), (0,)), ((), ())), preferred_element_type=jnp.float32
        )
        hidden_bias_grad = jnp.sum(grad_inner.astype(jnp.float32), axis=0)
        grad_features = lax.dot_general(
            grad_inner,
            hidden_weight[layer],
            (((1,), (1,)), ((), ())),
            preferred_element_type=jnp.float32,
        ).astype(jnp.bfloat16)
        sent = (
            jnp.zeros((tiles * capacity, channels), jnp.bfloat16)
            .at[target]
            .set(grad_features)
            .reshape(tiles, capacity, channels)
        )
        arrived = lax.all_to_all(sent, "tile", split_axis=0, concat_axis=0, tiled=True)
        local_grad = jnp.zeros((voxels, channels), jnp.float32)
        for spread_source in range(tiles):
            local_grad = local_grad + lax.dot_general(
                trilinear(received[:, spread_source], shape),
                arrived[spread_source],
                (((0,), (0,)), ((), ())),
                preferred_element_type=jnp.float32,
            )
        grad_updated = grad_current + lax.psum(local_grad.astype(jnp.bfloat16), "ray").astype(
            jnp.float32
        )
        conv_out = convolve_rows(padded, conv_weight[layer], shape, voxels)
        centred = (conv_out - mean) * inverse
        normal = centred * norm_gain[layer] + norm_shift[layer]
        sigma = jax.nn.sigmoid(normal)
        grad_normal = grad_updated * sigma * (1.0 + normal * (1.0 - sigma))
        partial_grads = (jnp.sum(grad_normal, axis=0), jnp.sum(grad_normal * centred, axis=0))
        grad_sum, grad_dot = lax.psum((partial_grads[0], partial_grads[1]), "tile")
        grad_conv_rows = (
            inverse
            * norm_gain[layer]
            * (grad_normal - grad_sum / every_voxel - centred * grad_dot / every_voxel)
        ).astype(jnp.bfloat16)
        grad_padded = pad_inner(padded_2(grad_conv_rows.reshape(shape), (("tile", 0),), 1))
        grad_current = grad_updated + convolve_back_rows(
            grad_padded, conv_weight[layer], shape, voxels
        )
        part_rows = voxels // lax.axis_size("ray")
        part_start = lax.axis_index("ray") * part_rows
        grad_part = lax.dynamic_slice_in_dim(grad_conv_rows, part_start, part_rows, 0)
        conv_term = weight_terms(padded, grad_part, part_start, shape)
        conv_total, hidden_weight_total, hidden_bias_total, head_weight_total, head_bias_total = (
            lax.psum(
                (conv_term, hidden_weight_grad, hidden_bias_grad, head_weight_grad, head_bias_grad),
                ("ray", "tile"),
            )
        )
        conv_grads[layer] = conv_total
        gain_grads[layer] = grad_dot
        shift_grads[layer] = grad_sum
        hidden_weight_grads[layer] = hidden_weight_total
        hidden_bias_grads[layer] = hidden_bias_total
        head_weight_grads[layer] = head_weight_total
        head_bias_grads[layer] = head_bias_total
    head_weight_all = jnp.stack(head_weight_grads)
    head_bias_all = jnp.stack(head_bias_grads)
    return (
        jnp.stack(pictures),
        rounded,
        grad_current.reshape(shape),
        jnp.stack(conv_grads),
        jnp.stack(gain_grads),
        jnp.stack(shift_grads),
        jnp.stack(hidden_weight_grads),
        jnp.stack(hidden_bias_grads),
        head_weight_all[:, :, classes],
        head_bias_all[:, classes],
        head_weight_all[:, :, :classes],
        head_bias_all[:, :classes],
    )


def solution(mesh):
    in_specs = (
        P("tile", None, None, None),
        P(("ray", "tile"), None),
        P(None, ("ray", "tile"), None),
        P(("ray", "tile"), None),
        P(("ray", "tile"), None),
        P(),
        P(),
        P(),
        P(),
        P(),
        P(),
        P(),
        P(),
        P(),
        P(None, ("ray", "tile"), None),
        P("tile", None, None, None),
    )
    out_specs = (
        P(None, ("ray", "tile"), None),
        P("tile", None, None, None),
        P("tile", None, None, None),
        P(),
        P(),
        P(),
        P(),
        P(),
        P(),
        P(),
        P(),
        P(),
    )
    return jax.shard_map(
        per_device, mesh=mesh, in_specs=in_specs, out_specs=out_specs, check_vma=False
    )
```

profile of v0, /device:TPU:0, one launch (start us, length us, event | category | flops | bytes accessed | tf_op | source)
XLA Modules:
  0.0 944.2 jit_solution(7454672845362089275)
XLA Ops:
  8.9 4.9 collective-permute-start
  21.3 6.2 scatter_fusion
  28.6 6.6 all-to-all-start
  55.0 8.4 fusion.480
  106.2 11.1 %all-reduce.9 = (f32[256]{0:T(256)S(1)}, f32[256]{0:T(256)S(1)}) all-reduce(f32[256]{0:T(256)S(1)} %get-tuple-element.67, f32[256]{0:T(256)S(1)} %get-tuple-element.66), channel_id=1, replica_groups=mesh['ray'=8,'tile'=4] {'tile'}, use_global_device_ids=true, to_apply=%region_7.8 | all-reduce | flops 512 | bytes 4096 | tf_op jit(solution)/shard_map/psum | solution.py:148
  122.6 5.6 collective-permute-start.2
  136.3 4.4 all-to-all-start.1
  145.4 8.4 fusion.478
  196.1 12.3 %all-reduce.8 = (f32[256]{0:T(256)S(1)}, f32[256]{0:T(256)S(1)}) all-reduce(f32[256]{0:T(256)S(1)} %get-tuple-element.65, f32[256]{0:T(256)S(1)} %get-tuple-element.64), channel_id=1, replica_groups=mesh['ray'=8,'tile'=4] {'tile'}, use_global_device_ids=true, to_apply=%region_15.16 | all-reduce | flops 512 | bytes 4096 | tf_op jit(solution)/shard_map/psum | solution.py:148
  209.1 4.0 add_convert_fusion
  221.6 4.8 all-to-all-start.2
  228.6 10.0 %gather_fusion = bf16[2048,256]{1,0:T(8,128)(2,1)} fusion(bf16[3072,256]{1,0:T(8,128)(2,1)} %bitcast.74, s32[2048]{0:T(1024)S(1)} %broadcast_clamp_fusion), kind=kCustom, calls=%fused_computation | custom fusion | bytes 2105344 | tf_op jit(solution)/shard_map/gather | solution.py:166
  246.7 10.9 %all-to-all-done.2 = bf16[4,768,256]{2,1,0:T(8,128)(2,1)} async-done(((bf16[4,768,256]{2,1,0:T(8,128)(2,1)}), bf16[4,768,256]{2,1,0:T(8,128)(2,1)}, u32[]{:S(2)}, u32[]{:S(2)}) %all-to-all-start.2) | async-done | bytes 1572896 | tf_op jit(solution)/shard_map/all_to_all | solution.py:163
  257.6 10.0 %gather_fusion.1 = bf16[2048,256]{1,0:T(8,128)(2,1)} fusion(bf16[3072,256]{1,0:T(8,128)(2,1)} %bitcast.145, s32[2048]{0:T(1024)S(1)} %broadcast_clamp_fusion), kind=kCustom, calls=%fused_computation.1 | custom fusion | bytes 2105344 | tf_op jit(solution)/shard_map/gather | solution.py:166
  282.5 11.0 %scatter_custom_fusion.4 = bf16[3072,256]{1,0:T(8,128)(2,1)} fusion(s32[2048]{0:T(1024)S(1)} %bitcast.1206, bf16[2048,256]{1,0:T(8,128)(2,1)} %convolution_convert_fusion, bf16[]{:T(256)} %constant.120.clone.1), kind=kCustom, calls=%fused_computation.315 | custom fusion | bytes 1573376 | tf_op jit(solution)/shard_map/scatter | solution.py:260
  293.4 16.1 %all-to-all-start.4 = ((bf16[4,768,256]{2,1,0:T(8,128)(2,1)}), bf16[4,768,256]{2,1,0:T(8,128)(2,1)}, u32[]{:S(2)}, u32[]{:S(2)}) async-start(bf16[4,768,256]{2,1,0:T(8,128)(2,1)} %bitcast.1018), calls=%async_computation.4 | async-start | bytes 3145728 | tf_op jit(solution)/shard_map/all_to_all | solution.py:263
  314.8 11.0 %scatter_custom_fusion.3 = bf16[3072,256]{1,0:T(8,128)(2,1)} fusion(s32[2048]{0:T(1024)S(1)} %bitcast.1207, bf16[2048,256]{1,0:T(8,128)(2,1)} %convolution_convert_fusion.1, bf16[]{:T(256)} %constant.120.clone.1), kind=kCustom, calls=%fused_computation.317 | custom fusion | bytes 1573376 | tf_op jit(solution)/shard_map/scatter | solution.py:260
  325.8 18.0 %all-to-all-done.4 = bf16[4,768,256]{2,1,0:T(8,128)(2,1)} async-done(((bf16[4,768,256]{2,1,0:T(8,128)(2,1)}), bf16[4,768,256]{2,1,0:T(8,128)(2,1)}, u32[]{:S(2)}, u32[]{:S(2)}) %all-to-all-start.4) | async-done | bytes 1572896 | tf_op jit(solution)/shard_map/all_to_all | solution.py:263
  343.8 4.4 all-to-all-start.3
  355.0 50.2 %all-reduce.4 = (f32[1,256]{1,0:T(1,128)S(1)}, f32[1,256]{1,0:T(1,128)S(1)}, f32[1,256,19]{1,2,0:T(8,128)S(1)}, f32[1,256,19]{1,2,0:T(8,128)S(1)}, f32[1,19]{1,0:T(1,128)S(1)}, /*index=5*/f32[1,19]{1,0:T(1,128)S(1)}) all-reduce(f32[1,256]{1,0:T(1,128)S(1)} %bitcast.1243, ...), channel_id=1, replica_groups=mesh['ray'=8,'tile'=4] {'ray','tile'}, use_global_device_ids=true, to_apply=%region_45.46 | all-reduce | flops 10278 | bytes 82224 | tf_op jit(solution)/shard_map/psum | solution.py:296
  407.3 4.2 fusion.86
  439.4 51.1 %all-reduce.16.cloned.1.call-done = (bf16[2048,256]{1,0:T(8,128)(2,1)}, bf16[2048,256]{1,0:T(8,128)(2,1)}) async-done(((bf16[2048,256]{1,0:T(8,128)(2,1)}, bf16[2048,256]{1,0:T(8,128)(2,1)}), (bf16[2048,256]{1,0:T(8,128)(2,1)}, bf16[2048,256]{1,0:T(8,128)(2,1)})) %all-reduce.16.cloned.1.call-update) | async-done | bytes 2097168 | tf_op jit(solution)/shard_map/psum | solution.py:272
  490.5 4.2 fusion.467
  494.7 11.9 %all-reduce.7 = (f32[256]{0:T(256)S(1)}, f32[256]{0:T(256)S(1)}) all-reduce(f32[256]{0:T(256)S(1)} %get-tuple-element.63, f32[256]{0:T(256)S(1)} %get-tuple-element.62), channel_id=1, replica_groups=mesh['ray'=8,'tile'=4] {'tile'}, use_global_device_ids=true, to_apply=%region_28.29 | all-reduce | flops 512 | bytes 4096 | tf_op jit(solution)/shard_map/psum | solution.py:281
  510.0 4.6 collective-permute-start.4
  551.3 9.0 fusion.476
  600.2 4.7 fusion.466
  604.8 8.3 all-reduce.6
  618.5 4.7 collective-permute-start.6
  675.4 8.8 fusion.474
  725.8 198.5 %all-reduce.14.cloned.1.call-done = (f32[1,27,256,256]{3,2,1,0:T(8,128)}, f32[1,27,256,256]{3,2,1,0:T(8,128)}, f32[1,256,256]{2,1,0:T(8,128)}, f32[1,256,256]{2,1,0:T(8,128)}) async-done(((f32[1,27,256,256]{3,2,1,0:T(8,128)}, f32[1,27,256,256]{3,2,1,0:T(8,128)}, f32[1,256,256]{2,1,0:T(8,128)}, f32[1,256,256]{2,1,0:T(8,128)}), (f32[1,27,256,256]{3,2,1,0:T(8,128)}, f32[1,27,256,256]{3,2,1,0:T(8,128)}, ...) | async-done | bytes 14680080 | tf_op jit(solution)/shard_map/psum | solution.py:296
  924.3 12.0 %pad_maximum_fusion = f32[2,27,256,256]{3,2,1,0:T(8,128)} fusion(f32[1,27,256,256]{3,2,1,0:T(8,128)} %get-tuple-element.98, f32[1,27,256,256]{3,2,1,0:T(8,128)} %get-tuple-element.99), kind=kLoop, calls=%fused_computation.9 | loop fusion | flops 3538944 | bytes 28311552 | tf_op jit(solution)/shard_map/stack | solution.py:314
  (697 shorter events, 385.9 us)
Async XLA Ops:
  8.9 41.3 %collective-permute-start = (bf16[1,16,16,256]{3,2,1,0:T(8,128)(2,1)}, bf16[1,16,16,256]{3,2,1,0:T(8,128)(2,1)S(1)}, u32[]{:S(2)}, u32[]{:S(2)}) collective-permute-start(bf16[1,16,16,256]{3,2,1,0:T(8,128)(2,1)} %get-tuple-element.234), channel_id=1, source_target_pairs={{0,1},{1,2},{2,3},{4,5},{5,6},{6,7},{8,9},{9,10},{10,11},{12,13},{... | collective-permute-start | bytes 393224 | tf_op jit(solution)/shard_map/ppermute | solution.py:19
  13.8 36.4 %collective-permute-start.1 = (bf16[1,16,16,256]{3,2,1,0:T(8,128)(2,1)}, bf16[1,16,16,256]{3,2,1,0:T(8,128)(2,1)}, u32[]{:S(2)}, u32[]{:S(2)}) collective-permute-start(bf16[1,16,16,256]{3,2,1,0:T(8,128)(2,1)} %get-tuple-element.235), channel_id=1, source_target_pairs={{1,0},{2,1},{3,2},{5,4},{6,5},{7,6},{9,8},{10,9},{11,10},{13,12},{... | collective-permute-start | bytes 393224 | tf_op jit(solution)/shard_map/ppermute | solution.py:20
  20.3 16.6 %copy-start.149 = (bf16[2,16,19]{2,1,0:T(8,128)(2,1)S(1)}, bf16[2,16,19]{2,1,0:T(8,128)(2,1)}, u32[]{:S(2)}) copy-start(bf16[2,16,19]{2,1,0:T(8,128)(2,1)} %param.30) | copy-start | bytes 3652
  28.6 12.4 %all-to-all-start = ((f32[6,4,768]{2,0,1:T(8,128)}), f32[6,4,768]{2,0,1:T(8,128)S(1)}, u32[]{:S(2)}, u32[]{:S(2)}) async-start(f32[6,4,768]{2,0,1:T(8,128)} %copy.57), calls=%async_computation | async-start | bytes 196608 | tf_op jit(solution)/shard_map/all_to_all | solution.py:137
  63.4 40.0 %copy-start.16 = (bf16[8,16,16,256]{3,2,1,0:T(8,128)(2,1)}, bf16[8,16,16,256]{3,2,1,0:T(8,128)(2,1)S(1)}, u32[]{:S(2)}) copy-start(bf16[8,16,16,256]{3,2,1,0:T(8,128)(2,1)S(1)} %get-tuple-element.196) | copy-start | bytes 3145732
  73.7 25.4 %copy-start.24 = (bf16[8,16,16,256]{3,2,1,0:T(8,128)(2,1)}, bf16[8,16,16,256]{3,2,1,0:T(8,128)(2,1)S(1)}, u32[]{:S(2)}) copy-start(bf16[8,16,16,256]{3,2,1,0:T(8,128)(2,1)S(1)} %get-tuple-element.232) | copy-start | bytes 3145732
  117.8 91.2 %copy-start.130 = (f32[256]{0:T(256)}, f32[256]{0:T(256)S(1)}, u32[]{:S(2)}) copy-start(f32[256]{0:T(256)S(1)} %get-tuple-element.247) | copy-start | bytes 3076
  121.3 19.4 %collective-permute-start.3 = (bf16[1,16,16,256]{3,2,1,0:T(8,128)(2,1)}, bf16[1,16,16,256]{3,2,1,0:T(8,128)(2,1)S(1)}, u32[]{:S(2)}, u32[]{:S(2)}) collective-permute-start(bf16[1,16,16,256]{3,2,1,0:T(8,128)(2,1)} %bitcast.85), channel_id=1, source_target_pairs={{1,0},{2,1},{3,2},{5,4},{6,5},{7,6},{9,8},{10,9},{11,10},{13,12},{... | collective-permute-start | bytes 393224 | tf_op jit(solution)/shard_map/ppermute | solution.py:20
  122.6 18.1 %collective-permute-start.2 = (bf16[1,16,16,256]{3,2,1,0:T(8,128)(2,1)}, bf16[1,16,16,256]{3,2,1,0:T(8,128)(2,1)}, u32[]{:S(2)}, u32[]{:S(2)}) collective-permute-start(bf16[1,16,16,256]{3,2,1,0:T(8,128)(2,1)} %bitcast.83), channel_id=1, source_target_pairs={{0,1},{1,2},{2,3},{4,5},{5,6},{6,7},{8,9},{9,10},{10,11},{12,13},{... | collective-permute-start | bytes 393224 | tf_op jit(solution)/shard_map/ppermute | solution.py:19
  136.3 85.3 %all-to-all-start.1 = ((bf16[4,768,256]{2,1,0:T(8,128)(2,1)}), bf16[4,768,256]{2,1,0:T(8,128)(2,1)}, u32[]{:S(2)}, u32[]{:S(2)}) async-start(bf16[4,768,256]{2,1,0:T(8,128)(2,1)} %pad_maximum_fusion.1), calls=%async_computation.1 | async-start | bytes 3145728 | tf_op jit(solution)/shard_map/all_to_all | solution.py:163
  153.9 22.1 %copy-start.21 = (bf16[8,16,16,256]{3,2,1,0:T(8,128)(2,1)}, bf16[8,16,16,256]{3,2,1,0:T(8,128)(2,1)S(1)}, u32[]{:S(2)}) copy-start(bf16[8,16,16,256]{3,2,1,0:T(8,128)(2,1)S(1)} %get-tuple-element.175) | copy-start | bytes 3145732
  153.9 39.4 %copy-start.20 = (bf16[8,16,16,256]{3,2,1,0:T(8,128)(2,1)}, bf16[8,16,16,256]{3,2,1,0:T(8,128)(2,1)S(1)}, u32[]{:S(2)}) copy-start(bf16[8,16,16,256]{3,2,1,0:T(8,128)(2,1)S(1)} %get-tuple-element.172) | copy-start | bytes 3145732
  162.4 26.6 %copy-start.26 = (bf16[8,16,16,256]{3,2,1,0:T(8,128)(2,1)}, bf16[8,16,16,256]{3,2,1,0:T(8,128)(2,1)S(1)}, u32[]{:S(2)}) copy-start(bf16[8,16,16,256]{3,2,1,0:T(8,128)(2,1)S(1)} %get-tuple-element.228) | copy-start | bytes 3145732
  221.6 36.1 %all-to-all-start.2 = ((bf16[4,768,256]{2,1,0:T(8,128)(2,1)}), bf16[4,768,256]{2,1,0:T(8,128)(2,1)}, u32[]{:S(2)}, u32[]{:S(2)}) async-start(bf16[4,768,256]{2,1,0:T(8,128)(2,1)} %pad_maximum_fusion.2), calls=%async_computation.2 | async-start | bytes 3145728 | tf_op jit(solution)/shard_map/all_to_all | solution.py:163
  228.5 45.2 %copy-start.151 = (f32[16]{0:T(128)}, f32[16]{0:T(128)S(1)}, u32[]{:S(2)}) copy-start(f32[16]{0:T(128)S(1)} %get-tuple-element.291) | copy-start | bytes 196
  228.5 43.1 %copy-start.155 = (bf16[256,1]{0,1:T(2,128)(2,1)}, bf16[256,1]{0,1:T(2,128)(2,1)S(1)}, u32[]{:S(2)}) copy-start(bf16[256,1]{0,1:T(2,128)(2,1)S(1)} %get-tuple-element.259) | copy-start | bytes 1540
  282.5 27.4 %copy-start.150 = (f32[16]{0:T(128)S(1)}, f32[16]{0:T(128)}, u32[]{:S(2)}) copy-start(f32[16]{0:T(128)} %get-tuple-element.292) | copy-start | bytes 196
  282.5 27.4 %copy-start.158 = (f32[16]{0:T(128)S(1)}, f32[16]{0:T(128)}, u32[]{:S(2)}) copy-start(f32[16]{0:T(128)} %get-tuple-element.117) | copy-start | bytes 196
  293.4 50.4 %all-to-all-start.4 = ((bf16[4,768,256]{2,1,0:T(8,128)(2,1)}), bf16[4,768,256]{2,1,0:T(8,128)(2,1)}, u32[]{:S(2)}, u32[]{:S(2)}) async-start(bf16[4,768,256]{2,1,0:T(8,128)(2,1)} %bitcast.1018), calls=%async_computation.4 | async-start | bytes 3145728 | tf_op jit(solution)/shard_map/all_to_all | solution.py:263
  325.8 26.0 %copy-start.119 = (bf16[2048,18]{0,1:T(8,128)(2,1)S(1)}, bf16[2048,18]{0,1:T(8,128)(2,1)}, u32[]{:S(2)}) copy-start(bf16[2048,18]{0,1:T(8,128)(2,1)} %copy-done.118) | copy-start | bytes 221188
  343.8 67.7 %all-to-all-start.3 = ((bf16[4,768,256]{2,1,0:T(8,128)(2,1)}), bf16[4,768,256]{2,1,0:T(8,128)(2,1)}, u32[]{:S(2)}, u32[]{:S(2)}) async-start(bf16[4,768,256]{2,1,0:T(8,128)(2,1)} %bitcast.1017), calls=%async_computation.3 | async-start | bytes 3145728 | tf_op jit(solution)/shard_map/all_to_all | solution.py:263
  348.2 142.3 %all-reduce.16.cloned.1.call-start = ((), (), s32[]{:S(2)}) async-start(), calls=%async_computation.6 | async-start | bytes 4194304 | tf_op jit(solution)/shard_map/psum | solution.py:272
  429.0 495.3 %all-reduce.14.cloned.1.call-start = ((), (), s32[]{:S(2)}) async-start(), calls=%async_computation.5 | async-start | bytes 29360128 | tf_op jit(solution)/shard_map/psum | solution.py:296
  434.0 56.5 %copy-start.9 = (f32[2048,256]{1,0:T(8,128)S(1)}, f32[2048,256]{1,0:T(8,128)}, u32[]{:S(2)}) copy-start(f32[2048,256]{1,0:T(8,128)} %get-tuple-element.265) | copy-start | bytes 6291460
  434.0 56.5 %copy-start.136 = (f32[256]{0:T(256)S(1)}, f32[256]{0:T(256)}, u32[]{:S(2)}) copy-start(f32[256]{0:T(256)} %copy-done.135) | copy-start | bytes 3076
  434.0 56.5 %copy-start.138 = (f32[256]{0:T(256)S(1)}, f32[256]{0:T(256)}, u32[]{:S(2)}) copy-start(f32[256]{0:T(256)} %copy-done.137) | copy-start | bytes 3076
  434.0 56.5 %copy-start.143 = (f32[1,256]{1,0:T(1,128)S(1)}, f32[1,256]{1,0:T(1,128)}, u32[]{:S(2)}) copy-start(f32[1,256]{1,0:T(1,128)} %get-tuple-element.252) | copy-start | bytes 3076
  434.0 56.5 %copy-start.148 = (f32[1,256]{1,0:T(1,128)S(1)}, f32[1,256]{1,0:T(1,128)}, u32[]{:S(2)}) copy-start(f32[1,256]{1,0:T(1,128)} %get-tuple-element.254) | copy-start | bytes 3076
  508.7 36.5 %collective-permute-start.5 = (bf16[1,16,16,256]{3,2,1,0:T(8,128)(2,1)S(1)}, bf16[1,16,16,256]{3,2,1,0:T(8,128)(2,1)S(1)}, u32[]{:S(2)}, u32[]{:S(2)}) collective-permute-start(bf16[1,16,16,256]{3,2,1,0:T(8,128)(2,1)S(1)} %bitcast.1194), channel_id=1, source_target_pairs={{1,0},{2,1},{3,2},{5,4},{6,5},{7,6},{9,8},{10,9},{11,10},{13,12},{... | collective-permute-start | bytes 393224 | tf_op jit(solution)/shard_map/ppermute | solution.py:20
  510.0 35.3 %collective-permute-start.4 = (bf16[1,16,16,256]{3,2,1,0:T(8,128)(2,1)S(1)}, bf16[1,16,16,256]{3,2,1,0:T(8,128)(2,1)S(1)}, u32[]{:S(2)}, u32[]{:S(2)}) collective-permute-start(bf16[1,16,16,256]{3,2,1,0:T(8,128)(2,1)S(1)} %bitcast.1193), channel_id=1, source_target_pairs={{0,1},{1,2},{2,3},{4,5},{5,6},{6,7},{8,9},{9,10},{10,11},{12,13},{... | collective-permute-start | bytes 393224 | tf_op jit(solution)/shard_map/ppermute | solution.py:19
  617.2 55.0 %collective-permute-start.7 = (bf16[1,16,16,256]{3,2,1,0:T(8,128)(2,1)S(1)}, bf16[1,16,16,256]{3,2,1,0:T(8,128)(2,1)S(1)}, u32[]{:S(2)}, u32[]{:S(2)}) collective-permute-start(bf16[1,16,16,256]{3,2,1,0:T(8,128)(2,1)S(1)} %bitcast.1192), channel_id=1, source_target_pairs={{1,0},{2,1},{3,2},{5,4},{6,5},{7,6},{9,8},{10,9},{11,10},{13,12},{... | collective-permute-start | bytes 393224 | tf_op jit(solution)/shard_map/ppermute | solution.py:20
  618.5 53.7 %collective-permute-start.6 = (bf16[1,16,16,256]{3,2,1,0:T(8,128)(2,1)S(1)}, bf16[1,16,16,256]{3,2,1,0:T(8,128)(2,1)S(1)}, u32[]{:S(2)}, u32[]{:S(2)}) collective-permute-start(bf16[1,16,16,256]{3,2,1,0:T(8,128)(2,1)S(1)} %bitcast.1191), channel_id=1, source_target_pairs={{0,1},{1,2},{2,3},{4,5},{5,6},{6,7},{8,9},{9,10},{10,11},{12,13},{... | collective-permute-start | bytes 393224 | tf_op jit(solution)/shard_map/ppermute | solution.py:19
  (154 other events, 588.6 us)
Sparse Core Ops, SparseCore 0:
  429.1 61.3 all-reduce.15
  671.7 252.5 all-reduce.13
where the time goes:
time: 952 us; the launch traced here: 944 us
  matrix products  299 us (31%)
  waiting for transfers between devices  280 us (29%)
  local copies, waits for them, and re-layouts  127 us (13%)
  blocking collectives  93.8 us (10%)
  other arithmetic  65.5 us (7%)
  starting transfers between devices  61.3 us (6%)
  between operations  18.1 us (2%)
    psum x1, waiting for transfers between devices, per_device(): lax.psum((conv_term, hidden_weight_grad, hidden_bias_grad, head_weight_gr...  198 us
    dot_general x54, matrix products, convolve_back_rows(): lax.dot_general(piece, weight[number], (((1,), (1,)), ((), ())), preferre...  83.5 us
    dot_general x54, matrix products, convolve_rows(): jnp.dot(piece, weight[number], preferred_element_type=jnp.float32)  80.2 us
    dot_general x54, matrix products, weight_terms(): lax.dot_general(piece, grad_rows, (((0,), (0,)), ((), ())), preferred_ele...  80.1 us
    psum x1, waiting for transfers between devices, per_device(): lax.psum(local_grad.astype(jnp.bfloat16), 'ray').astype(jnp.float32)  51.1 us
    psum x1, blocking collectives, per_device(): lax.psum((conv_term, hidden_weight_grad, hidden_bias_grad, head_weight_gr...  50.2 us
    slice x8, local copies, waits for them, and re-layouts, shifted(): padded[a:a + depth, b:b + height, c:c + width]  44.5 us
    psum x2, blocking collectives, per_device(): totals, squares = lax.psum((partial_stats[0], partial_stats[1]), 'tile')  23.3 us
  transfers between devices with their start and end apart: 15, of which 5 were waited for; matrix products, arithmetic and copies ran while one was open for 30% of the time, Pallas kernels for 0%

commit v1 on v0

v1 whole, which is shorter than its diff:
```python
import functools

import jax
import jax.numpy as jnp
from jax import lax
from jax.experimental import pallas as pl
from jax.experimental.pallas import tpu as pltpu
from jax.sharding import PartitionSpec as P

CAP = 768
WINDOW = 256
LANES = 128
PROWS = 24
DROWS = 32
COORDS = 8
BLOCKS = 8
PACK = 320
epsilon = 1e-05
MIB = 1024 * 1024

BF = jnp.bfloat16
F32 = jnp.float32
VMEM = pltpu.VMEM
SMEM = pltpu.SMEM


def nn(left, right):
    return jnp.dot(left, right, preferred_element_type=F32)


def nt(left, right):
    return lax.dot_general(left, right, (((1,), (1,)), ((), ())), preferred_element_type=F32)


def iota(shape, dim):
    return lax.broadcasted_iota(jnp.int32, shape, dim)


def whole(shape):
    return pl.BlockSpec(shape, lambda *_: (0,) * len(shape))


def planes_of(step, shape, first=0):
    return pl.BlockSpec((step,) + shape[1:], lambda i: (i + first // step,) + (0,) * (len(shape) - 1))


def sspec():
    return pl.BlockSpec(memory_space=SMEM)


def aspec():
    return pl.BlockSpec(memory_space=pl.ANY)


def hspec():
    return pl.BlockSpec(memory_space=pltpu.HBM)


def ordered(kernel, operands, in_specs, follow, **options):
    count, skip = len(operands), len(follow)

    def body(*refs):
        kernel(*refs[:count], *refs[count + skip :])

    return pl.pallas_call(body, in_specs=list(in_specs) + [aspec()] * skip, **options)(
        *operands, *follow
    )


def params(mib):
    return pltpu.CompilerParams(vmem_limit_bytes=int(mib * MIB))


def cost(flops, moved):
    return pl.CostEstimate(flops=int(flops), bytes_accessed=int(moved), transcendentals=0)


def lane_cumsum(x):
    lane = iota(x.shape, 1)
    shift = 1
    while shift < x.shape[1]:
        x = x + jnp.where(lane >= shift, pltpu.roll(x, shift, 1), 0.0)
        shift *= 2
    return x


def window_onehots(starts, owner_row, rank_row, ray, rays, tiles):
    rows = iota((WINDOW, rank_row.shape[1]), 0)
    hots, bases = [], []
    for t in range(tiles):
        start = starts[t * rays + ray]
        base = (start // LANES) * LANES
        place = jnp.where(owner_row == t, rank_row + (start - base), -1)
        hots.append((rows == place).astype(F32).astype(BF))
        bases.append(pl.multiple_of(base, LANES))
    return jnp.concatenate(hots, axis=0), bases


def prep_kernel(extent, starts, cells_ref, fracs_ref, out_ref, owner_ref, rank_ref, vals, acc):
    depth, height, width = extent
    tiles = out_ref.shape[0]
    rays, samples = cells_ref.shape
    cells = cells_ref[...]
    voxels = depth * height * width
    owner = lax.div(cells, voxels)
    local = cells - owner * voxels
    base_x = lax.div(local, height * width)
    inner = local - base_x * (height * width)
    base_y = lax.div(inner, width)
    base_z = inner - base_y * width
    rank = jnp.zeros(cells.shape, F32)
    for t in range(tiles):
        mine = owner == t
        rank = jnp.where(mine, lane_cumsum(jnp.where(mine, 1.0, 0.0)) - 1.0, rank)
    owner_ref[...] = owner
    rank_ref[...] = rank.astype(jnp.int32)
    vals[...] = jnp.zeros_like(vals)
    rows = [(base_x + 1).astype(F32), base_y.astype(F32), base_z.astype(F32)]
    low = []
    for d in range(3):
        frac = fracs_ref[d]
        high = frac.astype(BF).astype(F32)
        rows.append(high)
        low.append(frac - high)
    rows += low
    for number, row in enumerate(rows):
        for k in range(rays):
            vals[number : number + 1, k * samples : (k + 1) * samples] = row[k : k + 1]
    acc[...] = jnp.zeros_like(acc)
    for k in range(rays):
        hot, bases = window_onehots(
            starts, owner_ref[k : k + 1, :], rank_ref[k : k + 1, :], k, rays, tiles
        )
        moved = nt(vals[:, k * samples : (k + 1) * samples].astype(BF), hot)
        for t in range(tiles):
            acc[t, :, pl.ds(bases[t], WINDOW)] += moved[:, t * WINDOW : (t + 1) * WINDOW]
    out_ref[...] = jnp.zeros_like(out_ref)
    wide = out_ref.shape[2]
    lines = CAP // wide
    for n in range(lines):
        part = slice(n * wide, (n + 1) * wide)
        for r in range(6):
            value = acc[:, r : r + 1, part]
            if r >= 3:
                value = value + acc[:, r + 3 : r + 4, part]
            out_ref[:, r * lines + n : r * lines + n + 1, :] = value


def prepare(extent, starts, cells, fracs, tiles, wide, follow=()):
    rays, samples = cells.shape
    outs = ((tiles, COORDS * CAP // wide, wide), (rays, samples), (rays, samples))
    return ordered(
        functools.partial(prep_kernel, extent),
        (starts, cells, fracs,),
        [sspec(), whole(cells.shape), whole(fracs.shape)],
        follow,
        grid=(1,),
        out_shape=(
            jax.ShapeDtypeStruct(outs[0], F32),
            jax.ShapeDtypeStruct(outs[1], jnp.int32),
            jax.ShapeDtypeStruct(outs[2], jnp.int32),
        ),
        out_specs=tuple(whole(s) for s in outs),
        scratch_shapes=[VMEM((16, rays * samples), F32), VMEM((tiles, 16, CAP + WINDOW), F32)],
        compiler_params=params(60),
        cost_estimate=cost(4e8, 1e6),
        name="prep",
    )


def started(source, target, sem):
    copy = pltpu.make_async_copy(source, target, sem)
    copy.start()
    return copy


def put_plane(xs, p, value, width):
    rows, channels = value.shape
    along = lax.rem(iota(value.shape, 0), width)
    left = jnp.where(along == 0, 0.0, pltpu.roll(value, 1, 0))
    right = jnp.where(along == width - 1, 0.0, pltpu.roll(value, rows - 1, 0))
    xs[p, width : width + rows, 0:channels] = left.astype(BF)
    xs[p, width : width + rows, channels : 2 * channels] = value.astype(BF)
    xs[p, width : width + rows, 2 * channels : 3 * channels] = right.astype(BF)


def clear_edges(xs, width, rows):
    planes, _, wide = xs.shape
    for p in range(planes):
        xs[p, 0:width, :] = jnp.zeros((width, wide), BF)
        xs[p, width + rows : 2 * width + rows, :] = jnp.zeros((width, wide), BF)


def taps(xs, p, width, rows):
    return jnp.concatenate(
        [xs[p + a, b * width : b * width + rows, :] for a in range(3) for b in range(3)], axis=1
    )


def tap_pair(xs, first, width, rows):
    return jnp.concatenate(
        [taps(xs, first, width, rows), taps(xs, first + 1, width, rows)], axis=0
    )


def add_stats(sums, one, two):
    sums[0:1, :] += jnp.sum(one, axis=0, keepdims=True)
    sums[1:2, :] += jnp.sum(two, axis=0, keepdims=True)


def conv_scratch(planes, rows, width, channels, turned):
    shape = (channels, 27 * channels) if turned else (27 * channels, channels)
    return [VMEM((planes, rows + 2 * width, 3 * channels), BF), VMEM(shape, BF)]


def sems(*counts):
    return [pltpu.SemaphoreType.DMA((n,)) for n in counts]


def any_outs(*shapes):
    return tuple(jax.ShapeDtypeStruct(shape, dtype) for shape, dtype in shapes)


def conv_first_kernel(
    width, layer, before, own, after, coords, w_hbm, y_ref, v_ref, mix_ref,
    raw, xs, weight, y_buf, mix, in_sem, out_sem,
):
    planes, rows, channels = own.shape
    pairs = planes // 2 + 1
    body = [
        started(own.at[pl.ds(2 * i, 2)], raw.at[pl.ds(2 * i + 2, 2)], in_sem.at[i])
        for i in range(planes // 2)
    ]
    ends = [
        started(before, raw.at[pl.ds(0, 2)], in_sem.at[pairs]),
        started(after, raw.at[pl.ds(planes + 2, 2)], in_sem.at[pairs + 1]),
    ]
    heavy = started(w_hbm.at[layer], weight, in_sem.at[pairs + 2])
    light = started(coords, mix.at[:, pl.ds(8, coords.shape[1]), :], in_sem.at[pairs + 3])
    clear_edges(xs, width, rows)
    mix[:, 0:8, :] = jnp.zeros((mix.shape[0], 8, channels), F32)
    for copy in body + ends:
        copy.wait()

    @pl.loop(0, planes + 4)
    def _(p):
        put_plane(xs, p, raw[p].astype(F32), width)

    done = [started(raw.at[pl.ds(1, planes + 2)], v_ref, out_sem.at[pairs])]
    light.wait()
    heavy.wait()

    def out_copy(i):
        two = pl.ds(2 * i, 2)
        return pltpu.make_async_copy(y_buf.at[two], y_ref.at[two], out_sem.at[i])

    @pl.loop(0, pairs)
    def _(i):
        p = 2 * i
        part = nn(tap_pair(xs, p, width, rows), weight[...])
        y_buf[p] = part[:rows]
        y_buf[p + 1] = part[rows:]
        out_copy(i).start()
        for side, outer in ((0, 0), (1, pairs - 1)):

            @pl.when(i != outer)
            def _():
                kept = part[side * rows : (side + 1) * rows]
                add_stats(mix.at[0], kept, kept * kept)

    for t in range(1, mix.shape[0]):
        mix[t, 0:8, :] = mix[0, 0:8, :]
    done.append(started(mix, mix_ref, out_sem.at[pairs + 1]))
    for copy in done:
        copy.wait()
    for i in range(pairs):
        out_copy(i).wait()


def conv_first(before, own, after, coords, weights, layer, width):
    planes, rows, channels = own.shape
    ext = (planes + 2, rows, channels)
    tiles, lines, _ = coords.shape
    pairs = planes // 2 + 1
    return ordered(
        functools.partial(conv_first_kernel, width, layer),
        (before, own, after, coords, weights),
        [aspec()] * 5,
        (),
        out_shape=any_outs((ext, F32), (ext, BF), ((tiles, 8 + lines, channels), F32)),
        out_specs=(aspec(),) * 3,
        scratch_shapes=[VMEM((planes + 4, rows, channels), BF)]
        + conv_scratch(planes + 4, rows, width, channels, False)
        + [VMEM(ext, F32), VMEM((tiles, 8 + lines, channels), F32)]
        + sems(pairs + 4, pairs + 2),
        compiler_params=params(60),
        cost_estimate=cost(2 * 27 * channels * channels * rows * (planes + 2), 8e6),
        name="conv_first",
    )


def moments(total, count):
    both = jnp.sum(total, axis=0)
    mean = both[0:1, :] / count
    return mean, lax.rsqrt(both[1:2, :] / count - mean * mean + epsilon)


def row_of(ref, layer):
    return ref[layer : layer + 1, :]


def silu(value):
    return value * (1.0 / (1.0 + jnp.exp(-value)))


def conv_next_kernel(
    width, layer, count, flags, y_ext, v_ext, total_hbm, gain_hbm, shift_hbm, w_hbm,
    v_ref, r_ref, y_ref, stat_ref, first_ref, last_ref,
    y_in, v_in, total, gain, shift, xs, weight, v_buf, r_buf, y_buf, edges, stat, in_sem, out_sem,
):
    ext_planes, rows, channels = y_ext.shape
    pairs = ext_planes // 2
    small = [
        started(total_hbm.at[:, pl.ds(0, 8), :], total, in_sem.at[2 * pairs]),
        started(gain_hbm, gain, in_sem.at[2 * pairs + 1]),
        started(shift_hbm, shift, in_sem.at[2 * pairs + 2]),
    ]
    def in_copies(i):
        two = pl.ds(2 * i, 2)
        return (
            pltpu.make_async_copy(y_ext.at[two], y_in.at[two], in_sem.at[2 * i]),
            pltpu.make_async_copy(v_ext.at[two], v_in.at[two], in_sem.at[2 * i + 1]),
        )

    def mid_copies(i):
        two = pl.ds(2 * i, 2)
        return (
            pltpu.make_async_copy(v_buf.at[two], v_ref.at[two], out_sem.at[3 * i]),
            pltpu.make_async_copy(r_buf.at[two], r_ref.at[two], out_sem.at[3 * i + 1]),
        )

    def out_copy(i):
        two = pl.ds(2 * i - 2, 2)
        return pltpu.make_async_copy(y_buf.at[two], y_ref.at[two], out_sem.at[3 * i + 2])

    for i in range(pairs):
        for copy in in_copies(i):
            copy.start()
    heavy = started(w_hbm.at[layer + 1], weight, in_sem.at[2 * pairs + 3])
    clear_edges(xs, width, rows)
    stat[...] = jnp.zeros_like(stat)
    for copy in small:
        copy.wait()
    mean, inverse = moments(total[...], count)
    gains, shifts = row_of(gain, layer), row_of(shift, layer)

    @pl.loop(0, pairs)
    def _(i):
        for copy in in_copies(i):
            copy.wait()
        for side in range(2):
            p = 2 * i + side
            fresh = v_in[p].astype(F32) + silu((y_in[p] - mean) * inverse * gains + shifts)
            v_buf[p] = fresh
            outside = (p == side * (ext_planes - 1)) & (flags[side] == 0)
            rounded = jnp.where(outside, 0.0, fresh).astype(BF)
            r_buf[p] = rounded
            put_plane(xs, p, rounded.astype(F32), width)
        for copy in mid_copies(i):
            copy.start()

        @pl.when(i == 1)
        def _():
            heavy.wait()

        @pl.when(i > 0)
        def _():
            p = 2 * i - 2
            part = nn(tap_pair(xs, p, width, rows), weight[...])
            y_buf[p] = part[:rows]
            y_buf[p + 1] = part[rows:]
            add_stats(stat.at[0], part, part * part)
            out_copy(i).start()

    edges[0] = y_buf[0].astype(BF)
    edges[1] = y_buf[ext_planes - 3].astype(BF)
    for t in range(1, stat.shape[0]):
        stat[t] = stat[0]
    done = [
        started(stat, stat_ref, out_sem.at[2]),
        started(edges.at[pl.ds(0, 1)], first_ref, out_sem.at[3 * pairs]),
        started(edges.at[pl.ds(1, 1)], last_ref, out_sem.at[3 * pairs + 1]),
    ]
    for i in range(pairs):
        done += list(mid_copies(i)) + ([out_copy(i)] if i else [])
    for copy in done:
        copy.wait()


def conv_next(flags, y_ext, v_ext, total, gain, shift, weights, layer, width, count, follow=()):
    ext_planes, rows, channels = y_ext.shape
    ext = y_ext.shape
    inner = (ext_planes - 2, rows, channels)
    stat = (total.shape[0], 8, channels)
    pairs = ext_planes // 2
    edge = (1, rows, channels)
    return ordered(
        functools.partial(conv_next_kernel, width, layer, count),
        (flags, y_ext, v_ext, total, gain, shift, weights),
        [sspec()] + [aspec()] * 6,
        follow,
        out_shape=any_outs((ext, F32), (ext, BF), (inner, F32), (stat, F32), (edge, BF), (edge, BF)),
        out_specs=(aspec(),) * 6,
        scratch_shapes=[VMEM(ext, F32), VMEM(ext, BF), VMEM(stat, F32)]
        + [VMEM(gain.shape, F32)] * 2
        + conv_scratch(ext_planes, rows, width, channels, False)
        + [VMEM(ext, F32), VMEM(ext, BF), VMEM(inner, F32)]
        + [VMEM((2, rows, channels), BF), VMEM(stat, F32)]
        + sems(2 * pairs + 4, 3 * pairs + 2),
        compiler_params=params(60),
        cost_estimate=cost(2 * 27 * channels * channels * rows * (ext_planes - 2), 16e6),
        name="conv_next",
    )


def fill_weights(table, coords, extent):
    depth, height, width = extent
    samples = coords[0].shape[1]

    def along(base, frac, size):
        grid = iota((size, samples), 0).astype(F32)
        lower = jnp.where(grid == base, 1.0 - frac, 0.0)
        return lower + jnp.where(grid == base + 1.0, frac, 0.0)

    on_x = along(coords[0] - 1.0, coords[3], depth)
    on_y = along(coords[1], coords[4], height)
    on_z = along(coords[2], coords[5], width)
    for x in range(depth):
        on_xy = on_x[x : x + 1] * on_y
        for y in range(height):
            row = (x * height + y) * width
            table[row : row + width, :] = (on_xy[y : y + 1] * on_z).astype(BF)


def diagonal(rows, columns):
    return iota((rows, columns), 0) == iota((rows, columns), 1)


def identity(rows, columns):
    return diagonal(rows, columns).astype(F32).astype(BF)


def head_rows(semantic, density, rows):
    channels, classes = semantic.shape
    turned = nt(identity(rows, classes), semantic)
    return jnp.where(iota((rows, channels), 0) == classes, density.astype(F32), turned).astype(BF)


def column(row, rows):
    return jnp.sum(jnp.where(diagonal(rows, row.shape[1]), row, 0.0), axis=1, keepdims=True)


def coord_rows(block, slots):
    lines = slots // block.shape[1]
    return [
        jnp.concatenate(
            [block[8 + r * lines + n : 9 + r * lines + n, :] for n in range(lines)], axis=1
        )
        for r in range(6)
    ]


def sample_kernel(
    extent, layer, first, count, coords, *refs
):
    if count is None:
        r_hbm, refs = refs[0], refs[1:]
    else:
        y_hbm, v_hbm, total_hbm, gain, shift, refs = refs[0], refs[1], refs[2], refs[3], refs[4], refs[5:]
    hidden, hidden_b, semantic, density, semantic_b, density_b, refs = *refs[:6], refs[6:]
    p_ref, f_ref, g_ref, s_ref, refs = *refs[:4], refs[4:]
    if count is not None:
        r_out, refs = refs[0], refs[1:]
    turned, table, rounded, hidden_t, bias, head_t, head_b, sem, refs = *refs[:8], refs[8:]
    channels = turned.shape[0]
    depth = extent[0]
    classes = semantic.shape[2]
    slots = table.shape[1]
    rows = rounded.shape[1]
    step = pl.program_id(0)

    if count is not None:
        y_in, v_in, total, load_sem = refs

    def in_copies(p):
        return (
            pltpu.make_async_copy(y_hbm.at[p], y_in.at[p], load_sem.at[2 * p]),
            pltpu.make_async_copy(v_hbm.at[p + 1], v_in.at[p], load_sem.at[2 * p + 1]),
        )

    def out_copy(p):
        return pltpu.make_async_copy(rounded.at[p], r_out.at[p], sem.at[p])

    @pl.when(step == 0)
    def _():
        if count is None:
            copy = started(r_hbm.at[pl.ds(first, depth)], rounded, sem.at[0])
        else:
            light = started(total_hbm, total, load_sem.at[2 * depth])
            for p in range(depth):
                for copy in in_copies(p):
                    copy.start()
        same = identity(channels, channels)
        hidden_t[...] = nt(same, hidden[layer]).astype(BF)
        bias[...] = column(hidden_b[layer : layer + 1, :], channels)
        head_t[...] = head_rows(semantic[layer], density[layer : layer + 1, :], PROWS)
        last = jnp.sum(
            jnp.where(iota((1, density_b.shape[1]), 1) == layer, density_b[...], 0.0),
            axis=1,
            keepdims=True,
        )
        place = iota((PROWS, 1), 0) == classes
        head_b[...] = jnp.where(place, last, column(semantic_b[layer : layer + 1, :], PROWS))
        if count is None:
            copy.wait()
        else:
            light.wait()
            mean, inverse = moments(total[...], count)
            gains, shifts = row_of(gain, layer), row_of(shift, layer)

        @pl.loop(0, depth)
        def _(p):
            if count is not None:
                for copy in in_copies(p):
                    copy.wait()
                fresh = v_in[p] + silu((y_in[p] - mean) * inverse * gains + shifts)
                rounded[p] = fresh.astype(BF)
                out_copy(p).start()
            turned[:, pl.ds(pl.multiple_of(p * rows, rows), rows)] = nt(same, rounded[p]).astype(BF)

    fill_weights(table, coord_rows(coords[0], slots), extent)
    feature = nn(turned[...], table[...]).astype(BF)
    f_ref[0] = feature
    inner = nn(hidden_t[...], feature) + bias[...]
    small = jnp.exp(-jnp.abs(inner))
    act = (jnp.maximum(inner, 0.0) + jnp.log1p(small)).astype(BF)
    g_ref[0] = act
    s_ref[0] = jnp.where(inner >= 0.0, 1.0, small) / (1.0 + small)
    p_ref[0] = nn(head_t[...], act) + head_b[...]
    if count is not None:

        @pl.when(step == pl.num_programs(0) - 1)
        def _():
            for p in range(depth):
                out_copy(p).wait()


def per_tile(rows, lanes):
    return pl.BlockSpec((1, rows, lanes), lambda t: (t, 0, 0))


def sample(extent, received, source, layer, mlp, count=None, follow=()):
    tiles, lines, wide = received.shape
    slots = CAP
    rows, channels = extent[1] * extent[2], mlp[0].shape[1]
    depth = extent[0]
    voxels = depth * rows
    outs = [((tiles, PROWS, slots), F32)] + [((tiles, channels, slots), d) for d in (BF, BF, F32)]
    out_specs = [per_tile(n, slots) for n in (PROWS, channels, channels, channels)]
    scratch = [
        VMEM((channels, voxels), BF),
        VMEM((voxels, slots), BF),
        VMEM((depth, rows, channels), BF),
        VMEM((channels, channels), BF),
        VMEM((channels, 1), F32),
        VMEM((PROWS, channels), BF),
        VMEM((PROWS, 1), F32),
    ] + sems(depth)
    if count is None:
        first, given, specs = source[1], source[:1], [aspec()]
    else:
        first, given = 0, source
        specs = [aspec()] * 3 + [whole(x.shape) for x in source[3:]]
        outs.append(((depth, rows, channels), BF))
        out_specs.append(aspec())
        scratch += [VMEM((depth, rows, channels), F32)] * 2 + [VMEM(source[2].shape, F32)]
        scratch += sems(2 * depth + 1)
    return ordered(
        functools.partial(sample_kernel, extent, layer, first, count),
        (received,) + tuple(given) + mlp,
        [per_tile(lines, wide)] + specs + [whole(x.shape) for x in mlp],
        follow,
        grid=(tiles,),
        out_shape=any_outs(*outs),
        out_specs=tuple(out_specs),
        scratch_shapes=scratch,
        compiler_params=params(60),
        cost_estimate=cost(2 * voxels * channels * tiles * slots, 8e6),
        name="sample",
    )


def sample_back_kernel(
    extent, layer, coords, dp_ref, f_ref, g_ref, s_ref, hidden, semantic, density, *refs
):
    du_ref, pack_ref, total, table, head = refs[-5:]
    step = pl.program_id(0)
    channels = hidden.shape[1]
    slots = table.shape[1]

    @pl.when(step == 0)
    def _():
        total[...] = jnp.zeros_like(total)
        pack_ref[0:PACK, :] = jnp.zeros((PACK, channels), F32)
        if len(refs) > 5:
            pack_ref[PACK : 2 * PACK, :] = refs[0][...]
        rows = head_rows(semantic[layer], density[layer : layer + 1, :], DROWS)
        head[...] = nt(identity(channels, channels), rows).astype(BF)

    fill_weights(table, coord_rows(coords[0], slots), extent)
    grad_heads = dp_ref[0]
    grad_inner = (nn(head[...], grad_heads) * s_ref[0]).astype(BF)
    ones = jnp.ones((16, slots), BF)
    pack_ref[0:channels, :] += nt(f_ref[0], grad_inner)
    pack_ref[channels : channels + 16, :] += nt(ones, grad_inner)
    at = channels + 16
    pack_ref[at : at + DROWS, :] += nt(grad_heads, g_ref[0])
    at += DROWS
    pack_ref[at : at + 16, 0:DROWS] += nt(ones, grad_heads)
    grad_features = nn(hidden[layer], grad_inner).astype(BF)
    total[...] += nt(table[...], grad_features)

    @pl.when(step == pl.num_programs(0) - 1)
    def _():
        du_ref[...] = total[...].astype(BF)


def sample_back(extent, layer, received, grad_heads, feature, act, slope, mlp, packs, follow=()):
    tiles, lines, wide = received.shape
    _, channels, slots = feature.shape
    voxels = extent[0] * extent[1] * extent[2]
    hidden, _, semantic, density = mlp[:4]
    outs = ((voxels, channels), (PACK * (1 + len(packs)), channels))
    return ordered(
        functools.partial(sample_back_kernel, extent, layer),
        (received, grad_heads, feature, act, slope, hidden, semantic, density) + packs,
        [per_tile(lines, wide)]
        + [per_tile(n, slots) for n in (DROWS, channels, channels, channels)]
        + [whole(x.shape) for x in (hidden, semantic, density) + packs],
        follow,
        grid=(tiles,),
        out_shape=any_outs((outs[0], BF), (outs[1], F32)),
        out_specs=tuple(whole(shape) for shape in outs),
        scratch_shapes=[
            VMEM((voxels, channels), F32),
            VMEM((voxels, slots), BF),
            VMEM((channels, DROWS), BF),
        ],
        compiler_params=params(60),
        cost_estimate=cost(2 * voxels * channels * tiles * slots, 10e6),
        name="sample_back",
    )


def composite_kernel(
    classes, layer, starts, pixels, owner_ref, rank_ref, view, heads, cot,
    pic_ref, dp_ref, split, by_ray, grads, density, weights, grad_w, acc,
):
    tiles = heads.shape[0]
    rays, samples = owner_ref.shape
    step = 4.0 / samples
    split[...] = jnp.zeros_like(split)
    for t in range(tiles):
        value = heads[t]
        high = value.astype(BF)
        split[t, 0:PROWS, 0:CAP] = high.astype(F32)
        split[t, PROWS : 2 * PROWS, 0:CAP] = value - high.astype(F32)

    def hots(k):
        return window_onehots(
            starts, owner_ref[k : k + 1, :], rank_ref[k : k + 1, :], k, rays, tiles
        )

    for k in range(rays):
        hot, bases = hots(k)
        windows = jnp.concatenate(
            [split[t, :, pl.ds(bases[t], WINDOW)].astype(BF) for t in range(tiles)], axis=1
        )
        both = nn(windows, hot)
        one = both[:PROWS] + both[PROWS:]
        by_ray[k] = one
        density[k : k + 1, :] = one[classes : classes + 1]

    pre = density[...]
    visible = view[...].astype(F32)
    small = jnp.exp(-jnp.abs(pre))
    optical = visible * (jnp.maximum(pre, 0.0) + jnp.log1p(small)) * step
    passing = jnp.exp(-(lane_cumsum(optical) - optical))
    fading = jnp.exp(-optical)
    weight = passing * (1.0 - fading)
    weights[...] = weight
    row = iota((PROWS, samples), 0)
    lane = iota((PROWS, rays), 1)
    cotangent = nt(identity(PROWS, classes + 1), cot[layer])
    picture = jnp.zeros((PROWS, rays), F32)
    for k in range(rays):
        there = lane == pixels[k]
        dpic = jnp.sum(jnp.where(there, cotangent, 0.0), axis=1, keepdims=True)
        value = jnp.where(row < classes, by_ray[k], jnp.where(row == classes, 1.0, 0.0))
        one = weights[k : k + 1, :]
        colour = jnp.sum(value * one, axis=1, keepdims=True)
        picture = jnp.where(there, colour, picture)
        grad_w[k : k + 1, :] = jnp.sum(value * dpic, axis=0, keepdims=True)
        grads[k] = dpic * one
    pic_ref[...] = picture
    grad_weight = grad_w[...]
    carried = grad_weight * weight
    later = jnp.sum(carried, axis=1, keepdims=True) - lane_cumsum(carried)
    grad_optical = grad_weight * passing * fading - later
    slope = jnp.where(pre >= 0.0, 1.0, small) / (1.0 + small)
    density[...] = grad_optical * visible * step * slope
    acc[...] = jnp.zeros_like(acc)
    zero = jnp.zeros((DROWS - PROWS, samples), F32)
    for k in range(rays):
        hot, bases = hots(k)
        grad = jnp.where(row == classes, density[k : k + 1, :], grads[k])
        moved = nt(jnp.concatenate([grad, zero], axis=0).astype(BF), hot)
        for t in range(tiles):
            acc[t, :, pl.ds(bases[t], WINDOW)] += moved[:, t * WINDOW : (t + 1) * WINDOW]
    for t in range(tiles):
        dp_ref[t] = acc[t, :, 0:CAP].astype(BF)


def composite(starts, pixels, owner, rank, view, heads, cot, layer, classes, follow=()):
    tiles, _, slots = heads.shape
    rays, samples = owner.shape
    outs = ((PROWS, rays), (tiles, DROWS, slots))
    return ordered(
        functools.partial(composite_kernel, classes, layer),
        (starts, pixels, owner, rank, view, heads, cot,),
        [sspec(), sspec()] + [whole(x.shape) for x in (owner, rank, view, heads, cot)],
        follow,
        grid=(1,),
        out_shape=(jax.ShapeDtypeStruct(outs[0], F32), jax.ShapeDtypeStruct(outs[1], BF)),
        out_specs=tuple(whole(s) for s in outs),
        scratch_shapes=[
            VMEM((tiles, 2 * PROWS, CAP + WINDOW), F32),
            VMEM((rays, PROWS, samples), F32),
            VMEM((rays, PROWS, samples), F32),
            VMEM((rays, samples), F32),
            VMEM((rays, samples), F32),
            VMEM((rays, samples), F32),
            VMEM((tiles, DROWS, CAP + WINDOW), F32),
        ],
        compiler_params=params(60),
        cost_estimate=cost(1e9, 1e6),
        name="composite",
    )


def add_kernel(parts, out_ref):
    total = parts[0].astype(F32)
    for n in range(1, parts.shape[0]):
        total = total + parts[n].astype(F32)
    total = total.astype(out_ref.dtype)
    for n in range(out_ref.shape[0]):
        out_ref[n] = total


def add_parts(parts, copies, follow=()):
    shape = (copies,) + parts.shape[1:]
    return ordered(
        add_kernel,
        (parts,),
        [whole(parts.shape)],
        follow,
        grid=(1,),
        out_shape=jax.ShapeDtypeStruct(shape, parts.dtype),
        out_specs=whole(shape),
        compiler_params=params(60),
        cost_estimate=cost(1e6, 2e6),
        name="add_parts",
    )


def hold_kernel(*refs):
    del refs


def hold(values, follow):
    return ordered(
        hold_kernel,
        values,
        [aspec()] * len(values),
        follow,
        out_shape=any_outs(*((x.shape, x.dtype) for x in values)),
        out_specs=(aspec(),) * len(values),
        input_output_aliases={n: n for n in range(len(values))},
        compiler_params=params(60),
        name="hold",
    )


def halve_kernel(value, left_ref, right_ref):
    half = left_ref.shape[-1]
    for t in range(value.shape[0]):
        left_ref[t] = value[t, :, :half]
        right_ref[t] = value[t, :, half:]


def halve(value, follow):
    shape = value.shape[:-1] + (value.shape[-1] // 2,)
    return ordered(
        halve_kernel,
        (value,),
        [whole(value.shape)],
        follow,
        grid=(1,),
        out_shape=(jax.ShapeDtypeStruct(shape, value.dtype),) * 2,
        out_specs=(whole(shape),) * 2,
        compiler_params=params(60),
        cost_estimate=cost(1e6, 1e6),
        name="halve",
    )


def all_to_all(value, axis):
    return lax.all_to_all(value, axis, split_axis=0, concat_axis=0, tiled=True)


def exchange(first, last):
    devices = lax.axis_size("tile")
    up = [(i, i + 1) for i in range(devices - 1)]
    down = [(i + 1, i) for i in range(devices - 1)]
    return lax.ppermute(last, "tile", up), lax.ppermute(first, "tile", down)


def ray_grid():
    chips = lax.axis_size("ray") // 2
    across = max(n for n in range(1, chips + 1) if chips % n == 0 and n * n <= chips)
    return chips // across, across


def from_ray(value, down, right, core):
    tall, wide = ray_grid()
    pairs = []
    for y in range(tall):
        for x in range(wide):
            for c in range(2):
                source = ((y + down) % tall * wide + (x + right) % wide) * 2 + (c + core) % 2
                pairs.append((source, (y * wide + x) * 2 + c))
    return lax.ppermute(value, "ray", pairs)


def stack_kernel(groups, *refs):
    count = sum(groups)
    outs = refs[count:]
    at = 0
    for out_ref, size in zip(outs, groups):
        for n in range(size):
            out_ref[n] = refs[at][...]
            at += 1


def stacks(groups, follow=()):
    flat = [x for group in groups for x in group]
    shapes = [(len(group),) + group[0].shape for group in groups]
    return ordered(
        functools.partial(stack_kernel, [len(group) for group in groups]),
        tuple(flat),
        [whole(x.shape) for x in flat],
        follow,
        grid=(1,),
        out_shape=any_outs(*((shape, flat[0].dtype) for shape in shapes)),
        out_specs=tuple(whole(shape) for shape in shapes),
        compiler_params=params(60),
        cost_estimate=cost(1e6, 1e6),
        name="stacks",
    )


def gather_ray(left, right, placed):
    tall, wide = ray_grid()
    a = [left] + [from_ray(left, 0, x, 0) for x in range(1, wide)]
    b = [right] + [from_ray(right, y, 0, 0) for y in range(1, tall)]
    a, b = stacks((a, b))
    a = [a] + [from_ray(a, y, 0, 0) for y in range(1, tall)]
    b = [b] + [from_ray(b, 0, x, 0) for x in range(1, wide)]
    (both,) = stacks((a + b,), follow=(placed,))
    both = both.reshape((2, tall * wide) + left.shape)
    return both, from_ray(both, 0, 0, 1)


def norm_grads(y, grad, mean, inverse, gains, shifts):
    centred = (y - mean) * inverse
    normal = centred * gains + shifts
    sigma = 1.0 / (1.0 + jnp.exp(-normal))
    return grad * sigma * (1.0 + normal * (1.0 - sigma)), centred


def finish_back(sums, edges, ups, spare, out_sem):
    rows = edges.shape[1] - 16
    value = sums[...]
    high = value.astype(BF).astype(F32)
    middle = (value - high).astype(BF).astype(F32)
    low = value - high - middle
    tail = jnp.concatenate([high[0:2], middle[0:2], low[0:2], jnp.zeros((10,) + high.shape[1:], F32)], axis=0)
    tail = tail.astype(BF)
    edges[0, rows:, :] = tail
    edges[1, rows:, :] = tail
    spare[...] = tail
    first_ref, last_ref, far_ref = ups
    copies = [
        started(edges.at[0], first_ref, out_sem.at[0]),
        started(edges.at[1], last_ref, out_sem.at[1]),
        started(spare, far_ref, out_sem.at[2]),
    ]
    for copy in copies:
        copy.wait()


def norm_back_kernel(
    layer, count, cot, local, y, total_hbm, gain_hbm, shift_hbm, first_ref, last_ref, far_ref,
    cot_in, local_in, y_in, total, gain, shift, edges, sums, spare, in_sem, out_sem,
):
    planes, rows, _ = cot.shape
    small = [
        started(total_hbm, total, in_sem.at[3 * planes]),
        started(gain_hbm, gain, in_sem.at[3 * planes + 1]),
        started(shift_hbm, shift, in_sem.at[3 * planes + 2]),
    ]

    def in_copies(p):
        return [
            pltpu.make_async_copy(source.at[p], target.at[p], in_sem.at[3 * p + n])
            for n, (source, target) in enumerate(((cot, cot_in), (local, local_in), (y, y_in)))
        ]

    for p in range(planes):
        for copy in in_copies(p):
            copy.start()
    sums[...] = jnp.zeros_like(sums)
    for copy in small:
        copy.wait()
    mean, inverse = moments(total[...], count)
    gains, shifts = row_of(gain, layer), row_of(shift, layer)

    @pl.loop(0, planes)
    def _(p):
        for copy in in_copies(p):
            copy.wait()
        grad = cot_in[p].astype(F32) + local_in[p].astype(F32)
        inner, centred = norm_grads(y_in[p], grad, mean, inverse, gains, shifts)
        add_stats(sums, inner, inner * centred)
        for side, edge in ((0, 0), (1, planes - 1)):

            @pl.when(p == edge)
            def _():
                edges[side, 0:rows, :] = inner.astype(BF)

    finish_back(sums, edges, (first_ref, last_ref, far_ref), spare, out_sem)


def back_shapes(rows, channels):
    return ((rows + 16, channels), BF), ((rows + 16, channels), BF), ((16, channels), BF)


def back_scratch(rows, channels):
    return [VMEM((2, rows + 16, channels), BF), VMEM((8, channels), F32), VMEM((16, channels), BF)]


def norm_back(cot, local, y, total, gain, shift, layer, count, follow=()):
    planes, rows, channels = local.shape
    return ordered(
        functools.partial(norm_back_kernel, layer, count),
        (cot, local, y, total, gain, shift),
        [aspec()] * 6,
        follow,
        out_shape=any_outs(*back_shapes(rows, channels)),
        out_specs=(aspec(),) * 3,
        scratch_shapes=[VMEM(x.shape, x.dtype) for x in (cot, local, y, total, gain, shift)]
        + back_scratch(rows, channels)
        + sems(3 * planes + 3, 3),
        compiler_params=params(60),
        cost_estimate=cost(1e7, 8e6),
        name="norm_back",
    )


def share_back(sent):
    first, last, far = sent
    tiles = lax.axis_size("tile")

    def move(value, by):
        return lax.ppermute(value, "tile", [(i, (i + by) % tiles) for i in range(tiles)])

    return (move(last, 1), move(first, tiles - 1)) + tuple(move(far, n) for n in range(2, tiles - 1))


def turn_kernel(width, block, r_ref, out_ref, turned):
    planes, rows, channels = r_ref.shape
    chosen = out_ref.shape[1]
    pick = iota((chosen, channels), 1) == iota((chosen, channels), 0) + block[0] * chosen
    pick = pick.astype(F32).astype(BF)
    place = iota((chosen, rows), 1)
    on_y, on_z = lax.div(place, width), lax.rem(place, width)
    height = rows // width
    for p in range(planes):
        turned[...] = nt(pick, r_ref[p])
        for b in range(3):
            for c in range(3):
                shift = (b - 1) * width + (c - 1)
                value = turned[...]
                if shift:
                    value = pltpu.roll(value, (-shift) % rows, 1)
                y, z = on_y + (b - 1), on_z + (c - 1)
                inside = (y >= 0) & (y < height) & (z >= 0) & (z < width)
                value = jnp.where(inside, value, 0.0).astype(BF)
                for a in range(3):
                    target = p - a
                    if 0 <= target < planes - 2:
                        out_ref[9 * a + 3 * b + c, :, target * rows : (target + 1) * rows] = value


def turn(block, rounded, width, blocks, follow=()):
    planes, rows, channels = rounded.shape
    chosen = channels // blocks
    shape = (27, chosen, (planes - 2) * rows)
    return ordered(
        functools.partial(turn_kernel, width),
        (block, rounded,),
        [sspec(), whole(rounded.shape)],
        follow,
        grid=(1,),
        out_shape=jax.ShapeDtypeStruct(shape, BF),
        out_specs=whole(shape),
        scratch_shapes=[VMEM((chosen, rows), F32)],
        compiler_params=params(60),
        cost_estimate=cost(1e8, 5e6),
        name="turn",
    )


def weight_grad_kernel(layer, count, first, parts, tiles, spots, taps_hbm, *refs):
    grads, refs = refs[:parts], refs[parts:]
    if first:
        y, refs = refs[0], refs[1:]
        y_before, y_after = y.at[pl.ds(0, 1)], y.at[pl.ds(y.shape[0] - 1, 1)]
    else:
        y, y_before, y_after, refs = refs[0], refs[1], refs[2], refs[3:]
    own_far, others, refs = refs[0], refs[1:tiles], refs[tiles:]
    total_hbm, gain_hbm, shift_hbm, refs = *refs[:3], refs[3:]
    dy_ref, wg_ref, back_ref, refs = *refs[:3], refs[3:]
    grads_in, refs = refs[:parts], refs[parts:]
    (taps_in, y_in, y_halo, dn_halo, rest, back, total, gain, shift, dy_buf, dy_rows, wg_buf, in_sem,
     out_sem) = refs
    planes, rows, channels = grads[0].shape
    spare = (parts + 1) * planes
    lists = [
        (total_hbm.at[:, pl.ds(0, 8), :], total),
        (gain_hbm, gain),
        (shift_hbm, shift),
        (y_before, y_halo.at[pl.ds(0, 1)]),
        (y_after, y_halo.at[pl.ds(1, 1)]),
        (others[0], dn_halo.at[0]),
        (others[1], dn_halo.at[1]),
        (own_far, rest.at[0]),
    ] + [(other, rest.at[n + 1]) for n, other in enumerate(others[2:])]
    small = [
        started(source, target, in_sem.at[spare + n]) for n, (source, target) in enumerate(lists)
    ]

    def in_copies(p):
        copies = [pltpu.make_async_copy(y.at[p + first], y_in.at[p], in_sem.at[(parts + 1) * p])]
        for n in range(parts):
            copies.append(
                pltpu.make_async_copy(
                    grads[n].at[p], grads_in[n].at[p], in_sem.at[(parts + 1) * p + 1 + n]
                )
            )
        return copies

    for p in range(planes):
        for copy in in_copies(p):
            copy.start()
    heavy = started(taps_hbm, taps_in, in_sem.at[spare + len(lists)])
    for copy in small:
        copy.wait()
    tile = spots[2]
    tails = [rest[0], dn_halo[0, rows:, :], dn_halo[1, rows:, :]]
    tails += [rest[n] for n in range(1, rest.shape[0])]
    for by, tail in zip([0, 1, tiles - 1] + list(range(2, tiles - 1)), tails):
        value = tail.astype(F32)
        value = value[0:2] + value[2:4] + value[4:6]
        back[lax.rem(tile + tiles - by, tiles), 0:2, :] = value
    mean, inverse = moments(total[...], count)
    gains, shifts = row_of(gain, layer), row_of(shift, layer)
    scale = inverse * gains
    both = back[0, 0:2, :]
    for t in range(1, tiles):
        both = both + back[t, 0:2, :]
    back[0, 0:2, :] = both
    sums = both / count

    def finish(inner, centred):
        return scale * (inner - sums[0:1, :] - centred * sums[1:2, :])

    for side, place in ((0, 0), (1, planes + 1)):
        centred = (y_halo[side].astype(F32) - mean) * inverse
        value = finish(dn_halo[side, 0:rows, :].astype(F32), centred)
        dy_buf[place] = jnp.where(spots[side] > 0, value, 0.0).astype(BF)

    @pl.loop(0, planes)
    def _(p):
        for copy in in_copies(p):
            copy.wait()
        grad = grads_in[0][p].astype(F32)
        for n in range(1, parts):
            grad = grad + grads_in[n][p].astype(F32)
        value = finish(*norm_grads(y_in[p], grad, mean, inverse, gains, shifts)).astype(BF)
        dy_buf[p + 1] = value
        dy_rows[pl.ds(pl.multiple_of(p * rows, rows), rows), :] = value

    done = [
        started(dy_buf, dy_ref, out_sem.at[0]),
        started(back.at[0, pl.ds(0, 2), :], back_ref, out_sem.at[2]),
    ]
    heavy.wait()
    wg_buf[...] = nn(taps_in[...], dy_rows[...]).astype(BF)
    done.append(started(wg_buf, wg_ref, out_sem.at[1]))
    for copy in done:
        copy.wait()


def weight_grad(
    spots, taps_t, grads, y, y_halo, far, others, total, gain, shift, layer, count
):
    planes, rows, channels = grads[0].shape
    wide = taps_t.shape[0]
    tiles = len(others) + 1
    ext = (planes + 2, rows, channels)
    own = (planes, rows, channels)
    operands = (taps_t,) + tuple(grads) + (y,) + tuple(y_halo) + (far,) + tuple(others)
    operands += (total, gain, shift)
    return ordered(
        functools.partial(weight_grad_kernel, layer, count, 0 if y_halo else 1, len(grads), tiles),
        (spots,) + operands,
        [sspec()] + [aspec()] * len(operands),
        (),
        out_shape=any_outs((ext, BF), ((wide, channels), BF), ((2, channels), F32)),
        out_specs=(aspec(),) * 3,
        scratch_shapes=[VMEM(x.shape, x.dtype) for x in grads]
        + [
            VMEM(taps_t.shape, BF),
            VMEM(own, F32),
            VMEM((2, rows, channels), BF if y_halo else F32),
            VMEM((2, rows + 16, channels), BF),
            VMEM((tiles - 2, 16, channels), BF),
            VMEM((tiles, 8, channels), F32),
            VMEM((tiles, 8, channels), F32),
            VMEM(gain.shape, F32),
            VMEM(gain.shape, F32),
            VMEM(ext, BF),
            VMEM((planes * rows, channels), BF),
            VMEM((wide, channels), BF),
        ]
        + sems((len(grads) + 1) * planes + 8 + tiles, 3),
        compiler_params=params(60),
        cost_estimate=cost(2 * wide * planes * rows * channels, 12e6),
        name="weight_grad",
    )


def conv_back_kernel(width, layer, count, parts, dy, w_hbm, *refs):
    more = count is not None
    grads, refs = refs[:parts], refs[parts:]
    if more:
        y, total_hbm, gain_hbm, shift_hbm, refs = *refs[:4], refs[4:]
    out_ref, refs = refs[0], refs[1:]
    if more:
        sent, refs = refs[:3], refs[3:]
    grads_in, refs = refs[:parts], refs[parts:]
    raw, xs, weight, out_buf, in_sem, w_sem, out_sem, refs = *refs[:7], refs[7:]
    ext_planes, rows, channels = dy.shape
    planes = ext_planes - 2
    pairs = planes // 2
    each = parts + 1
    body = started(dy, raw, in_sem.at[each * pairs])
    heavy = [
        started(
            w_hbm.at[layer, pl.ds((26 - o) * channels, channels), :],
            weight.at[:, pl.ds(o * channels, channels)],
            w_sem.at[o],
        )
        for o in range(27)
    ]
    small = []
    if more:
        y_in, total, gain, shift, edges, sums, spare, back_sem = refs
        small = [
            started(source, target, in_sem.at[each * pairs + 1 + n])
            for n, (source, target) in enumerate(
                ((total_hbm.at[:, pl.ds(0, 8), :], total), (gain_hbm, gain), (shift_hbm, shift))
            )
        ]
        sums[...] = jnp.zeros_like(sums)

    def in_copies(i):
        two = pl.ds(2 * i, 2)
        copies = [
            pltpu.make_async_copy(grads[n].at[two], grads_in[n].at[two], in_sem.at[each * i + n])
            for n in range(parts)
        ]
        if more:
            copies.append(
                pltpu.make_async_copy(
                    y.at[pl.ds(2 * i + 1, 2)], y_in.at[two], in_sem.at[each * i + parts]
                )
            )
        return copies

    def out_copy(i):
        two = pl.ds(2 * i, 2)
        return pltpu.make_async_copy(out_buf.at[two], out_ref.at[two], out_sem.at[i])

    for i in range(pairs):
        for copy in in_copies(i):
            copy.start()
    clear_edges(xs, width, rows)
    body.wait()

    @pl.loop(0, ext_planes)
    def _(p):
        put_plane(xs, p, raw[p].astype(F32), width)

    for copy in small + heavy:
        copy.wait()
    if more:
        mean, inverse = moments(total[...], count)
        gains, shifts = row_of(gain, layer - 1), row_of(shift, layer - 1)

    @pl.loop(0, pairs)
    def _(i):
        part = nt(tap_pair(xs, 2 * i, width, rows), weight[...])
        for copy in in_copies(i):
            copy.wait()
        for side in range(2):
            p = 2 * i + side
            value = part[side * rows : (side + 1) * rows]
            for n in range(parts):
                value = value + grads_in[n][p].astype(F32)
            out_buf[p] = value
            if more:
                inner, centred = norm_grads(y_in[p], value, mean, inverse, gains, shifts)
                add_stats(sums, inner, inner * centred)

                @pl.when(p == side * (planes - 1))
                def _():
                    edges[side, 0:rows, :] = inner.astype(BF)

        out_copy(i).start()

    if more:
        finish_back(sums, edges, sent, spare, back_sem)
    for i in range(pairs):
        out_copy(i).wait()


def conv_back(dy, grads, weights, layer, width, norm=None, follow=()):
    ext_planes, rows, channels = dy.shape
    own = (ext_planes - 2, rows, channels)
    pairs = own[0] // 2
    outs, extra, scratch = [(own, F32)], (), []
    if norm is not None:
        y, total, gain, shift, count = norm
        extra = (y, total, gain, shift)
        outs += list(back_shapes(rows, channels))
        scratch = [VMEM(own, F32), VMEM((total.shape[0], 8, channels), F32)]
        scratch += [VMEM(gain.shape, F32), VMEM(gain.shape, F32)]
        scratch += back_scratch(rows, channels) + sems(3)
    else:
        count = None
    return ordered(
        functools.partial(conv_back_kernel, width, layer, count, len(grads)),
        (dy, weights) + tuple(grads) + extra,
        [aspec()] * (2 + len(grads) + len(extra)),
        follow,
        out_shape=any_outs(*outs),
        out_specs=(aspec(),) * len(outs),
        scratch_shapes=[VMEM(x.shape, x.dtype) for x in grads]
        + [VMEM(dy.shape, BF)]
        + conv_scratch(ext_planes, rows, width, channels, True)
        + [VMEM(own, F32)]
        + sems(pairs * (len(grads) + 1) + 4, 27, pairs)
        + scratch,
        compiler_params=params(60),
        cost_estimate=cost(2 * 27 * channels * channels * rows * own[0], 10e6),
        name="conv_back",
    )


GROUP = 9


def place_kernel(part, out_ref):
    blocks, offsets, chosen, _ = part.shape
    for o in range(offsets):
        for b in range(blocks):
            out_ref[0, o, b * chosen : (b + 1) * chosen, :] = part[b, o].astype(F32)


def place(parts, layer, layers, follow=()):
    blocks, offsets, chosen, channels = parts.shape
    shape = (layers, offsets, blocks * chosen, channels)
    return ordered(
        place_kernel,
        (parts,),
        [pl.BlockSpec((blocks, GROUP, chosen, channels), lambda o: (0, o, 0, 0))],
        follow,
        grid=(offsets // GROUP,),
        out_shape=jax.ShapeDtypeStruct(shape, F32),
        out_specs=pl.BlockSpec((1, GROUP) + shape[2:], lambda o: (layer, o, 0, 0)),
        compiler_params=params(60),
        cost_estimate=cost(1e6, 11e6),
        name="place",
    )


def place_near_kernel(tall, wide, blocks, spot, own, other, kept, out_ref):
    _, _, offsets, chosen, half = own.shape
    y, x, core = spot[0], spot[1], spot[2]
    for source, cross in ((own, 0), (other, 1)):
        for side in range(2):
            for n in range(tall * wide):
                down, right = (n // wide, n % wide) if side == 0 else (n % tall, n // tall)
                ray = lax.rem(y + down, tall) * wide + lax.rem(x + right, wide)
                ray = ray * 2 + lax.rem(core + cross, 2)
                row = pl.multiple_of(lax.rem(ray, blocks) * chosen, chosen)
                for o in range(offsets):
                    out_ref[0, o, pl.ds(row, chosen), side * half : (side + 1) * half] = source[
                        side, n, o
                    ].astype(F32)


def place_near(spot, own, other, kept, layer, blocks):
    _, rays, offsets, chosen, half = own.shape
    tall, wide = ray_grid()
    spec = pl.BlockSpec((2, rays, GROUP, chosen, half), lambda o: (0, 0, o, 0, 0))
    return pl.pallas_call(
        functools.partial(place_near_kernel, tall, wide, blocks),
        grid=(offsets // GROUP,),
        out_shape=jax.ShapeDtypeStruct(kept.shape, F32),
        in_specs=[sspec(), spec, spec, aspec()],
        out_specs=pl.BlockSpec((1, GROUP) + kept.shape[2:], lambda o: (layer, o, 0, 0)),
        input_output_aliases={3: 0},
        compiler_params=params(60),
        cost_estimate=cost(1e6, 11e6),
        name="place_near",
    )(spot, own, other, kept)


def per_device(
    volume,
    sample_cells,
    sample_fracs,
    view_mask,
    pixel_of_ray,
    conv_weight,
    norm_gain,
    norm_shift,
    hidden_weight,
    hidden_bias,
    density_weight,
    density_bias,
    semantic_weight,
    semantic_bias,
    render_cotangent,
    volume_cotangent,
):
    extent = volume.shape[:3]
    depth, height, width, channels = volume.shape
    rows = height * width
    voxels = depth * rows
    tiles = lax.axis_size("tile")
    ray_devices = lax.axis_size("ray")
    count = float(voxels * tiles)
    rays, samples = sample_cells.shape
    classes = semantic_weight.shape[2]
    layers = conv_weight.shape[0]
    blocks = min(BLOCKS, ray_devices)
    chosen = channels // blocks
    tile, ray = lax.axis_index("tile"), lax.axis_index("ray")
    block = lax.rem(ray, blocks).astype(jnp.int32).reshape(1)
    tall, wide = ray_grid()
    spot = jnp.stack([ray // (2 * wide), ray // 2 % wide, ray % 2]).astype(jnp.int32)

    own = volume.reshape(depth, rows, channels)
    before, after = exchange(own[:2], own[-2:])
    flags = jnp.stack([tile > 0, tile < tiles - 1]).astype(jnp.int32)

    owner_of = lax.div(sample_cells, voxels)
    held = owner_of[None] == jnp.arange(tiles, dtype=jnp.int32)[:, None, None]
    earlier = jnp.arange(rays)[None, :] < jnp.arange(rays)[:, None]
    starts = jnp.sum(
        (held[:, None, :, :] & earlier[None, :, :, None]).astype(jnp.int32), axis=(2, 3)
    ).reshape(tiles * rays)
    pixels = pixel_of_ray[0]
    buffer, owner, rank = prepare(extent, starts, sample_cells, sample_fracs, tiles, channels)

    weights = conv_weight.reshape(layers, 27 * channels, channels)
    mlp = (
        hidden_weight,
        hidden_bias,
        semantic_weight,
        density_weight,
        semantic_bias,
        density_bias[None],
    )
    y_ext, v_ext, mixed = conv_first(before, own, after, buffer, weights, 0, width)
    total = received = all_to_all(mixed, "tile")
    taps_first = turn(block, v_ext, width, blocks)
    v_next, r_ext, y_next, stat, y_first, y_last = conv_next(
        flags, y_ext, v_ext, total, norm_gain, norm_shift, weights, 0, width, count,
        follow=(taps_first,),
    )
    total_next = all_to_all(stat, "tile")
    heads, feature, act, slope = sample(extent, received, (r_ext, 1), 0, mlp)
    heads_last, feature_last, act_last, slope_last, r_last = sample(
        extent, received, (y_next, v_next, total_next, norm_gain, norm_shift), 1, mlp, count,
        follow=(heads,),
    )

    def draw(heads, layer, follow):
        return composite(
            starts, pixels, owner, rank, view_mask, all_to_all(heads, "tile"), render_cotangent,
            layer, classes, follow=follow,
        )

    picture, grad_heads = draw(heads, 0, (heads_last,))
    picture_last, grad_heads_last = draw(heads_last, 1, (grad_heads,))
    shares = (ray_devices, voxels // ray_devices, channels)
    planes = (depth, rows, channels)
    local, pack = sample_back(
        extent, 0, received, all_to_all(grad_heads, "tile"), feature, act, slope, mlp, (),
        follow=(grad_heads_last,),
    )
    parts = all_to_all(local.reshape(shares), "ray")
    local_last, packed = sample_back(
        extent, 1, received, all_to_all(grad_heads_last, "tile"), feature_last, act_last,
        slope_last, mlp, (pack,), follow=(local,),
    )
    parts_last = all_to_all(local_last.reshape(shares), "ray")
    copies = add_parts(parts, ray_devices, follow=(local_last,))
    (packed,) = hold((packed,), (copies,))
    packed = all_to_all(packed.reshape(ray_devices, -1, channels), "ray")
    copies_last = add_parts(parts_last, ray_devices, follow=(copies, local_last))
    sums_last = all_to_all(copies_last, "ray").reshape(planes)
    y_edges = exchange(*hold((y_first, y_last), (copies_last,)))
    packed = add_parts(packed, tiles, follow=(copies_last,))
    taps_next = turn(block, r_ext, width, blocks, follow=(packed,))

    cot = volume_cotangent.reshape(planes)
    wide_taps = (27 * chosen, voxels)
    spots = jnp.stack([tile > 0, tile < tiles - 1, tile]).astype(jnp.int32)
    sent = norm_back(
        cot, sums_last, y_next, total_next, norm_gain, norm_shift, 1, count,
        follow=(taps_next,) + y_edges,
    )
    (copies,) = hold((copies,), (sent[2],))
    sums = all_to_all(copies, "ray").reshape(planes)
    dy, part, back_last = weight_grad(
        spots, taps_next.reshape(wide_taps), (cot, sums_last), y_next, y_edges, sent[2],
        share_back(sent), total_next, norm_gain, norm_shift, 1, count,
    )
    shard = lax.psum_scatter(part, "tile", scatter_dimension=0, tiled=True)
    grad, *sent = conv_back(
        dy, (cot, sums_last, sums), weights, 1, width,
        (y_ext, total, norm_gain, norm_shift, count),
    )
    (shard,) = hold((shard,), (sent[2],))
    gathered = lax.all_gather(shard, ("ray", "tile"), axis=0, tiled=True)

    dy, part, back = weight_grad(
        spots, taps_first.reshape(wide_taps), (grad,), y_ext, (), sent[2], share_back(sent), total,
        norm_gain, norm_shift, 0, count,
    )
    parts = all_to_all(part.reshape(tiles, 27 * chosen // tiles, channels), "tile")
    packed = add_parts(all_to_all(packed, "tile"), ray_devices, follow=(part,))
    copies = add_parts(parts, tiles, follow=(packed,))
    slices = all_to_all(copies, "tile")
    (grad,) = conv_back(dy, (grad,), weights, 0, width, follow=(copies,))
    packed = all_to_all(packed, "ray").reshape(layers, PACK, channels)[::-1]
    left, right = halve(slices, (grad,))
    half = (27, chosen, channels // 2)
    gathered = gathered[: blocks * 27 * chosen].reshape(blocks, 27, chosen, channels)
    conv_grad = place(gathered, 1, layers, follow=(left,))
    near, far = gather_ray(left.reshape(half), right.reshape(half), conv_grad)
    conv_grad = place_near(spot, near, far, conv_grad, 0, blocks)

    at = channels + 16
    heads = packed[:, at : at + DROWS]
    head_bias = packed[:, at + DROWS, :DROWS]
    return (
        jnp.swapaxes(jnp.stack([picture, picture_last])[:, : classes + 1], 1, 2),
        r_last.reshape(volume.shape),
        grad.reshape(volume.shape),
        conv_grad,
        jnp.stack([back, back_last])[:, 1],
        jnp.stack([back, back_last])[:, 0],
        packed[:, :channels],
        packed[:, channels],
        heads[:, classes],
        head_bias[:, classes],
        jnp.swapaxes(heads[:, :classes], 1, 2),
        head_bias[:, :classes],
    )


def solution(mesh):
    in_specs = (
        P("tile", None, None, None),
        P(("ray", "tile"), None),
        P(None, ("ray", "tile"), None),
        P(("ray", "tile"), None),
        P(("ray", "tile"), None),
        P(),
        P(),
        P(),
        P(),
        P(),
        P(),
        P(),
        P(),
        P(),
        P(None, ("ray", "tile"), None),
        P("tile", None, None, None),
    )
    out_specs = (
        P(None, ("ray", "tile"), None),
        P("tile", None, None, None),
        P("tile", None, None, None),
        P(),
        P(),
        P(),
        P(),
        P(),
        P(),
        P(),
        P(),
        P(),
    )
    return jax.shard_map(
        per_device, mesh=mesh, in_specs=in_specs, out_specs=out_specs, check_vma=False
    )
```

time: 952 us -> 388 us (0.41)
  matrix products: 299 us -> 0 us
  waiting for transfers between devices: 280 us -> 97.8 us
  Pallas kernels: 0 us -> 168 us
  local copies, waits for them, and re-layouts: 127 us -> 16.4 us
  blocking collectives: 93.8 us -> 0 us
  other arithmetic: 65.5 us -> 3.89 us
  starting transfers between devices: 61.3 us -> 85.2 us
    dot_general x190 -> x0, matrix products: 299 us -> none  [the longest x54 83.5 us: convolve_back_rows(): lax.dot_general(piece, weight[number], (((1,), (1,)), ((), ())), preferre...]
    psum x2 -> x0, waiting for transfers between devices: 250 us -> none  [the longest x1 198 us: per_device(): lax.psum((conv_term, hidden_weight_grad, hidden_bias_grad, head_weight_gr...]
    pallas_call x0 -> x30, Pallas kernels: none -> 168 us  [the longest x29 163 us: ordered(): pl.pallas_call(body, in_specs=list(in_specs) + [aspec()] * skip, **options)]
    psum x5 -> x0, blocking collectives: 93.8 us -> none  [the longest x1 50.2 us: per_device(): lax.psum((conv_term, hidden_weight_grad, hidden_bias_grad, head_weight_gr...]
    slice x27 -> x11, local copies, waits for them, and re-layouts: 50.8 us -> 4.62 us  [the longest x1 1.07 us: per_device(): before, after = exchange(own[:2], own[-2:])]
    all_to_all x5 -> x15, waiting for transfers between devices: 30.1 us -> 62 us  [all_to_all(): return lax.all_to_all(value, axis, split_axis=0, concat_axis=0, tiled=True)]
    ppermute x8 -> x15, waiting for transfers between devices: 0.02 us -> 31.1 us  [the longest x6 18.1 us: move(): lax.ppermute(value, 'tile', [(i, (i + by) % tiles) for i in range(tiles)])]
    scatter x5 -> x0, local copies, waits for them, and re-layouts: 29.8 us -> none  [the longest x2 22 us: per_device(): sent = jnp.zeros((tiles * capacity, channels), jnp.bfloat16).at[target].s...]
  transfers between devices with their start and end apart: 15 -> 32, of which waited for: 5 -> 19; matrix products, arithmetic and copies ran while one was open for 30% -> 3% of each run, Pallas kernels for 0% -> 33%
where the time goes in v1:
time: 388 us; the launch traced here: 386 us
  Pallas kernels  168 us (43%)
  waiting for transfers between devices  97.8 us (25%)
  starting transfers between devices  85.2 us (22%)
  local copies, waits for them, and re-layouts  16.4 us (4%)
  between operations  14.6 us (4%)
  other arithmetic  3.89 us (1%)
    pallas_call x29, Pallas kernels, ordered(): pl.pallas_call(body, in_specs=list(in_specs) + [aspec()] * skip, **options)  163 us
    all_to_all x15, waiting for transfers between devices, all_to_all(): return lax.all_to_all(value, axis, split_axis=0, concat_axis=0, tiled=True)  62 us
    all_to_all x15, starting transfers between devices, all_to_all(): return lax.all_to_all(value, axis, split_axis=0, concat_axis=0, tiled=True)  58.2 us
    ppermute x6, waiting for transfers between devices, move(): lax.ppermute(value, 'tile', [(i, (i + by) % tiles) for i in range(tiles)])  18.1 us
    ppermute x4, starting transfers between devices, exchange(): return (lax.ppermute(last, 'tile', up), lax.ppermute(first, 'tile', down))  11.5 us
    unnamed x82, local copies, waits for them, and re-layouts  11.2 us
    ppermute x5, waiting for transfers between devices, from_ray(): return lax.ppermute(value, 'ray', pairs)  10 us
    ppermute x6, starting transfers between devices, move(): lax.ppermute(value, 'tile', [(i, (i + by) % tiles) for i in range(tiles)])  9.91 us
  transfers between devices with their start and end apart: 32, of which 19 were waited for; matrix products, arithmetic and copies ran while one was open for 3% of the time, Pallas kernels for 33%

profile of v1, /device:TPU:0, one launch (start us, length us, event | category | flops | bytes accessed | tf_op | source)
XLA Modules:
  0.0 385.6 jit_solution(2929323247688178293)
XLA Ops:
  8.2 4.9 %collective-permute-start = (bf16[2,256,256]{2,1,0:T(8,128)(2,1)S(1)}, bf16[2,256,256]{2,1,0:T(8,128)(2,1)S(1)}, u32[]{:S(2)}, u32[]{:S(2)}) collective-permute-start(bf16[2,256,256]{2,1,0:T(8,128)(2,1)S(1)} %bitcast.63), channel_id=1, source_target_pairs={{0,1},{1,2},{2,3},{4,5},{5,6},{6,7},{8,9},{9,10},{10,11},{12,13},{... | collective-permute-start | bytes 786440 | tf_op jit(solution)/shard_map/ppermute | solution.py:835
  23.6 13.8 %conv_first.1 = (f32[10,256,256]{2,1,0:T(8,128)}, bf16[10,256,256]{2,1,0:T(8,128)(2,1)}, f32[4,32,256]{2,1,0:T(8,128)}) custom-call(bf16[2,256,256]{2,1,0:T(8,128)(2,1)} %copy-done.34, bf16[8,256,256]{2,1,0:T(8,128)(2,1)} %bitcast.61, bf16[2,256,256]{2,1,0:T(8,128)(2,1)} %copy-done.35, f32[4,24,256]{2,1,0:T(8,128)} %get-tuple-element.62.refs_3_, ...), custom_call_target="tpu_custom_call" | custom-call | flops 9059696640 | bytes 8000000 | tf_op jit(solution)/shard_map/conv_first/pallas_call | solution.py:65
  47.8 15.0 %conv_next.1 = (f32[10,256,256]{2,1,0:T(8,128)}, bf16[10,256,256]{2,1,0:T(8,128)(2,1)}, f32[8,256,256]{2,1,0:T(8,128)}, f32[4,8,256]{2,1,0:T(8,128)}, bf16[1,256...) custom-call(s32[2]{0:T(128)} %add_convert_fusion.refs_0_, f32[10,256,256]{2,1,0:T(8,128)} %get-tuple-element.64.refs_1_.refs_5_.refs_3_, ...), custom_call_target="tpu_custom_call" | custom-call | flops 7247757312 | bytes 16000000 | tf_op jit(solution)/shard_map/conv_next/pallas_call | solution.py:65
  62.8 4.5 %all-to-all-start.2 = ((f32[4,8,256]{2,1,0:T(8,128)}), f32[4,8,256]{2,1,0:T(8,128)S(1)}, u32[]{:S(2)}, u32[]{:S(2)}) async-start(f32[4,8,256]{2,1,0:T(8,128)} %get-tuple-element.70), calls=%async_computation.2 | async-start | bytes 65536 | tf_op jit(solution)/shard_map/all_to_all | solution.py:828
  67.2 12.3 %sample.2 = (f32[4,24,768]{2,1,0:T(8,128)}, bf16[4,256,768]{2,1,0:T(8,128)(2,1)}, bf16[4,256,768]{2,1,0:T(8,128)(2,1)}, f32[4,256,768]{2,1,0:T(8,128)}) custom-call(f32[4,32,256]{2,1,0:T(8,128)} %copy-done.11, bf16[10,256,256]{2,1,0:T(8,128)(2,1)} %get-tuple-element.66.refs_1_, bf16[2,256,256]{2,1,0:T(8,128)(2,1)} %refs_5_.10, f32[2,256]{1,0:T(2,128)} %refs_7_.4, ...), custom_call_target="tpu_custom_call" | custom-call | flops 3221225472 | bytes 8000000 | tf_op jit(solution)/shard_map/sample/pallas_call | solution.py:65
  79.6 5.1 %all-to-all-start.1 = ((f32[4,24,768]{2,1,0:T(8,128)}), f32[4,24,768]{2,1,0:T(8,128)S(1)}, u32[]{:S(2)}, u32[]{:S(2)}) async-start(f32[4,24,768]{2,1,0:T(8,128)} %get-tuple-element.67.refs_12_), calls=%async_computation.1 | async-start | bytes 589824 | tf_op jit(solution)/shard_map/all_to_all | solution.py:828
  84.6 13.0 %sample.3 = (f32[4,24,768]{2,1,0:T(8,128)}, bf16[4,256,768]{2,1,0:T(8,128)(2,1)}, bf16[4,256,768]{2,1,0:T(8,128)(2,1)}, f32[4,256,768]{2,1,0:T(8,128)}, bf16[8,256,256]{2,1,0:T(8,128)(2,1)}) custom-call(f32[4,32,256]{2,1,0:T(8,128)} %copy-done.11, f32[8,256,256]{2,1,0:T(8,128)} %get-tuple-element.68.refs_1_.refs_2_.refs_4_, ...), custom_call_target="tpu_custom_call" | custom-call | flops 3221225472 | bytes 8000000 | tf_op jit(solution)/shard_map/sample/pallas_call | solution.py:65
  97.7 5.1 %all-to-all-start.3 = ((f32[4,24,768]{2,1,0:T(8,128)}), f32[4,24,768]{2,1,0:T(8,128)S(1)}, u32[]{:S(2)}, u32[]{:S(2)}) async-start(f32[4,24,768]{2,1,0:T(8,128)} %get-tuple-element.71.refs_7_), calls=%async_computation.3 | async-start | bytes 589824 | tf_op jit(solution)/shard_map/all_to_all | solution.py:828
  102.8 5.3 %composite.2 = (f32[24,16]{1,0:T(8,128)}, bf16[4,32,768]{2,1,0:T(8,128)(2,1)}) custom-call(s32[64]{0:T(128)} %reshape.97.refs_0_, s32[16]{0:T(128)} %bitcast.81, s32[16,128]{1,0:T(8,128)} %get-tuple-element.60.refs_2_, s32[16,128]{1,0:T(8,128)} %get-tuple-element.61.refs_3_, s32[16,128]{1,0:T(8,128)} %refs_4_.9, f32[4,24,768]{2,1,0:T(8,128)} %copy-done.15, ...), custom_call_target="tpu_custom_call" | custom-call | flops 1000000000 | bytes 1000000 | tf_op jit(solution)/shard_map/composite/pallas_call | solution.py:65
  113.4 5.3 %composite.3 = (f32[24,16]{1,0:T(8,128)}, bf16[4,32,768]{2,1,0:T(8,128)(2,1)}) custom-call(s32[64]{0:T(128)} %reshape.97.refs_0_, s32[16]{0:T(128)} %bitcast.82, s32[16,128]{1,0:T(8,128)} %get-tuple-element.60.refs_2_, s32[16,128]{1,0:T(8,128)} %get-tuple-element.61.refs_3_, s32[16,128]{1,0:T(8,128)} %refs_4_.9, f32[4,24,768]{2,1,0:T(8,128)} %copy-done.16, ...), custom_call_target="tpu_custom_call" | custom-call | flops 1000000000 | bytes 1000000 | tf_op jit(solution)/shard_map/composite/pallas_call | solution.py:65
  119.6 4.1 %all-to-all-start.4 = ((bf16[4,32,768]{2,1,0:T(8,128)(2,1)}), bf16[4,32,768]{2,1,0:T(8,128)(2,1)S(1)}, u32[]{:S(2)}, u32[]{:S(2)}) async-start(bf16[4,32,768]{2,1,0:T(8,128)(2,1)} %get-tuple-element.76.refs_8_), calls=%async_computation.4 | async-start | bytes 393216 | tf_op jit(solution)/shard_map/all_to_all | solution.py:828
  123.7 9.8 %sample_back.2 = (bf16[2048,256]{1,0:T(8,128)(2,1)}, f32[320,256]{1,0:T(8,128)}) custom-call(f32[4,32,256]{2,1,0:T(8,128)} %copy-done.11, bf16[4,32,768]{2,1,0:T(8,128)(2,1)} %copy-done.20, bf16[4,256,768]{2,1,0:T(8,128)(2,1)} %get-tuple-element.80.refs_2_, bf16[4,256,768]{2,1,0:T(8,128)(2,1)} %get-tuple-element.81.refs_3_, ...), custom_call_target="tpu_custom_call" | custom-call | flops 3221225472 | bytes 10000000 | tf_op jit(solution)/shard_map/sample_back/pallas_call | solution.py:65
  137.3 10.3 %sample_back.3 = (bf16[2048,256]{1,0:T(8,128)(2,1)}, f32[640,256]{1,0:T(8,128)}) custom-call(f32[4,32,256]{2,1,0:T(8,128)} %copy-done.11, bf16[4,32,768]{2,1,0:T(8,128)(2,1)} %copy-done.19, bf16[4,256,768]{2,1,0:T(8,128)(2,1)} %get-tuple-element.77.refs_2_, bf16[4,256,768]{2,1,0:T(8,128)(2,1)} %get-tuple-element.78.refs_3_, ...), custom_call_target="tpu_custom_call" | custom-call | flops 3221225472 | bytes 10000000 | tf_op jit(solution)/shard_map/sample_back/pallas_call | solution.py:65
  147.6 5.1 %all-to-all-done.6.refs_0_ = bf16[8,256,256]{2,1,0:T(8,128)(2,1)S(1)} async-done(((bf16[8,256,256]{2,1,0:T(8,128)(2,1)}), bf16[8,256,256]{2,1,0:T(8,128)(2,1)S(1)}, u32[]{:S(2)}, u32[]{:S(2)}) %all-to-all-start.6) | async-done | bytes 1048608 | tf_op jit(solution)/shard_map/all_to_all | solution.py:828
  158.7 12.9 %all-to-all-done.8.refs_0_ = bf16[8,256,256]{2,1,0:T(8,128)(2,1)S(1)} async-done(((bf16[8,256,256]{2,1,0:T(8,128)(2,1)}), bf16[8,256,256]{2,1,0:T(8,128)(2,1)S(1)}, u32[]{:S(2)}, u32[]{:S(2)}) %all-to-all-start.8) | async-done | bytes 1048608 | tf_op jit(solution)/shard_map/all_to_all | solution.py:828
  177.6 8.7 %all-to-all-done.7.refs_0_ = f32[8,80,256]{2,1,0:T(8,128)S(1)} async-done(((f32[8,80,256]{2,1,0:T(8,128)}), f32[8,80,256]{2,1,0:T(8,128)S(1)}, u32[]{:S(2)}, u32[]{:S(2)}) %all-to-all-start.7) | async-done | bytes 655392 | tf_op jit(solution)/shard_map/all_to_all | solution.py:828
  189.8 4.0 %collective-permute-start.2 = (bf16[1,256,256]{2,1,0:T(8,128)(2,1)}, bf16[1,256,256]{2,1,0:T(8,128)(2,1)S(1)}, u32[]{:S(2)}, u32[]{:S(2)}) collective-permute-start(bf16[1,256,256]{2,1,0:T(8,128)(2,1)} %get-tuple-element.89), channel_id=1, source_target_pairs={{0,1},{1,2},{2,3},{4,5},{5,6},{6,7},{8,9},{9,10},{10,11},{12,13},{... | collective-permute-start | bytes 393224 | tf_op jit(solution)/shard_map/ppermute | solution.py:835
  197.0 3.9 %turn.3.refs_6_ = bf16[27,32,2048]{2,1,0:T(8,128)(2,1)} custom-call(s32[1]{0:T(128)} %bitcast.7.refs_0_, bf16[10,256,256]{2,1,0:T(8,128)(2,1)} %get-tuple-element.66.refs_1_, f32[4,80,256]{2,1,0:T(8,128)} %add_parts.7.refs_2_), custom_call_target="tpu_custom_call" | custom-call | flops 100000000 | bytes 5000000 | tf_op jit(solution)/shard_map/turn/pallas_call | solution.py:65
  206.2 4.0 %norm_back.1 = (bf16[272,256]{1,0:T(8,128)(2,1)}, bf16[272,256]{1,0:T(8,128)(2,1)}, bf16[16,256]{1,0:T(8,128)(2,1)}) custom-call(bf16[8,256,256]{2,1,0:T(8,128)(2,1)} %bitcast.47, bf16[8,256,256]{2,1,0:T(8,128)(2,1)} %copy-done, f32[8,256,256]{2,1,0:T(8,128)} %get-tuple-element.68.refs_1_.refs_2_.refs_4_, f32[4,8,256]{2,1,0:T(8,128)} %copy-done.14, ...), custom_call_target="tpu_custom_call" | custom-call | flops 10000000 | bytes 8000000 | tf_op jit(solution)/shard_map/norm_back/pallas_call | solution.py:65
  219.6 5.8 %collective-permute-done.6.refs_10_ = bf16[16,256]{1,0:T(8,128)(2,1)S(1)} collective-permute-done((bf16[16,256]{1,0:T(8,128)(2,1)S(1)}, bf16[16,256]{1,0:T(8,128)(2,1)S(1)}, u32[]{:S(2)}, u32[]{:S(2)}) %collective-permute-start.6) | collective-permute-done | bytes 8224 | tf_op jit(solution)/shard_map/ppermute | solution.py:995
  226.2 6.5 %weight_grad.2 = (bf16[10,256,256]{2,1,0:T(8,128)(2,1)}, bf16[864,256]{1,0:T(8,128)(2,1)}, f32[2,256]{1,0:T(2,128)}) custom-call(s32[3]{0:T(128)} %pad_add_fusion.refs_0_, bf16[864,2048]{1,0:T(8,128)(2,1)} %bitcast.42, bf16[8,256,256]{2,1,0:T(8,128)(2,1)} %bitcast.48, bf16[8,256,256]{2,1,0:T(8,128)(2,1)} %copy-done, ...), custom_call_target="tpu_custom_call" | custom-call | flops 905969664 | bytes 12000000 | tf_op jit(solution)/shard_map/weight_grad/pallas_call | solution.py:65
  233.7 15.1 %conv_back.2 = (f32[8,256,256]{2,1,0:T(8,128)}, bf16[272,256]{1,0:T(8,128)(2,1)}, bf16[272,256]{1,0:T(8,128)(2,1)}, bf16[16,256]{1,0:T(8,128)(2,1)}) custom-call(bf16[10,256,256]{2,1,0:T(8,128)(2,1)} %get-tuple-element.94.refs_0_, bf16[2,6912,256]{2,1,0:T(8,128)(2,1)} %bitcast.77, bf16[8,256,256]{2,1,0:T(8,128)(2,1)} %bitcast.49, ...), custom_call_target="tpu_custom_call" | custom-call | flops 7247757312 | bytes 10000000 | tf_op jit(solution)/shard_map/conv_back/pallas_call | solution.py:65
  248.8 4.7 %reduce-scatter.2.cloned.1.call-done.refs_0_ = bf16[216,256]{1,0:T(8,128)(2,1)} async-done(((bf16[864,256]{1,0:T(8,128)(2,1)}), bf16[216,256]{1,0:T(8,128)(2,1)}) %reduce-scatter.2.cloned.1.call-update) | async-done | bytes 110608 | tf_op jit(solution)/shard_map/reduce_scatter | solution.py:1475
  261.8 12.3 %collective-permute-done.9.refs_7_ = bf16[16,256]{1,0:T(8,128)(2,1)S(1)} collective-permute-done((bf16[16,256]{1,0:T(8,128)(2,1)}, bf16[16,256]{1,0:T(8,128)(2,1)S(1)}, u32[]{:S(2)}, u32[]{:S(2)}) %collective-permute-start.9) | collective-permute-done | bytes 8224 | tf_op jit(solution)/shard_map/ppermute | solution.py:995
  274.9 6.4 %weight_grad.3 = (bf16[10,256,256]{2,1,0:T(8,128)(2,1)}, bf16[864,256]{1,0:T(8,128)(2,1)}, f32[2,256]{1,0:T(2,128)}) custom-call(s32[3]{0:T(128)} %pad_add_fusion.refs_0_, bf16[864,2048]{1,0:T(8,128)(2,1)} %bitcast.43, f32[8,256,256]{2,1,0:T(8,128)} %get-tuple-element.95.refs_2_, f32[10,256,256]{2,1,0:T(8,128)} %get-tuple-element.64.refs_1_.refs_5_.refs_3_, ...), custom_call_target="tpu_custom_call" | custom-call | flops 905969664 | bytes 12000000 | tf_op jit(solution)/shard_map/weight_grad/pallas_call | solution.py:65
  286.6 12.5 %all-to-all-done.11.refs_0_ = bf16[4,216,256]{2,1,0:T(8,128)(2,1)S(1)} async-done(((bf16[4,216,256]{2,1,0:T(8,128)(2,1)}), bf16[4,216,256]{2,1,0:T(8,128)(2,1)S(1)}, u32[]{:S(2)}, u32[]{:S(2)}) %all-to-all-start.11) | async-done | bytes 442400 | tf_op jit(solution)/shard_map/all_to_all | solution.py:828
  305.1 12.6 %conv_back.3.refs_1_ = f32[8,256,256]{2,1,0:T(8,128)} custom-call(bf16[10,256,256]{2,1,0:T(8,128)(2,1)} %get-tuple-element.99.refs_0_, bf16[2,6912,256]{2,1,0:T(8,128)(2,1)} %bitcast.78, f32[8,256,256]{2,1,0:T(8,128)} %get-tuple-element.95.refs_2_, bf16[4,216,256]{2,1,0:T(8,128)(2,1)} %add_parts.9.refs_3_), custom_call_target="tpu_custom_call" | custom-call | flops 7247757312 | bytes 10000000 | tf_op jit(solution)/shard_map/conv_back/pallas_call | solution.py:65
  317.8 6.4 %all-to-all-done.13.refs_0_ = bf16[4,216,256]{2,1,0:T(8,128)(2,1)S(1)} async-done(((bf16[4,216,256]{2,1,0:T(8,128)(2,1)}), bf16[4,216,256]{2,1,0:T(8,128)(2,1)S(1)}, u32[]{:S(2)}, u32[]{:S(2)}) %all-to-all-start.13) | async-done | bytes 442400 | tf_op jit(solution)/shard_map/all_to_all | solution.py:828
  329.8 4.3 %collective-permute-done.10.refs_1_ = bf16[27,32,128]{2,1,0:T(8,128)(2,1)S(1)} collective-permute-done((bf16[27,32,128]{2,1,0:T(8,128)(2,1)}, bf16[27,32,128]{2,1,0:T(8,128)(2,1)S(1)}, u32[]{:S(2)}, u32[]{:S(2)}) %collective-permute-start.10) | collective-permute-done | bytes 221216 | tf_op jit(solution)/shard_map/ppermute | solution.py:852
  340.8 5.2 %place.1.refs_4_.kept = f32[2,27,256,256]{3,2,1,0:T(8,128)} custom-call(bf16[8,27,32,256]{3,2,1,0:T(8,128)(2,1)} %bitcast.50, bf16[4,216,128]{2,1,0:T(8,128)(2,1)} %get-tuple-element.101.refs_1_), custom_call_target="tpu_custom_call" | custom-call | flops 1000000 | bytes 11000000 | tf_op jit(solution)/shard_map/place/pallas_call | solution.py:65
  359.5 9.1 %all-to-all-done.14 = f32[8,80,256]{2,1,0:T(8,128)S(1)} async-done(((f32[8,80,256]{2,1,0:T(8,128)}), f32[8,80,256]{2,1,0:T(8,128)S(1)}, u32[]{:S(2)}, u32[]{:S(2)}) %all-to-all-start.14) | async-done | bytes 655392 | tf_op jit(solution)/shard_map/all_to_all | solution.py:828
  373.5 5.2 %place_near.1 = f32[2,27,256,256]{3,2,1,0:T(8,128)} custom-call(s32[3]{0:T(128)} %pad_add_fusion.1.spot, bf16[2,4,27,32,128]{4,3,2,1,0:T(8,128)(2,1)} %bitcast.46, bf16[2,4,27,32,128]{4,3,2,1,0:T(8,128)(2,1)} %copy-done.6, f32[2,27,256,256]{3,2,1,0:T(8,128)} %place.1.refs_4_.kept), custom_call_target="tpu_custom_call", output_to_operand_aliasing={{}: (3, {})} | custom-call | flops 1000000 | bytes 11000000 | tf_op jit(solution)/shard_map/place_near/pallas_call | solution.py:1349
  (167 shorter events, 117.9 us)
Async XLA Ops:
  8.2 12.1 %collective-permute-start = (bf16[2,256,256]{2,1,0:T(8,128)(2,1)S(1)}, bf16[2,256,256]{2,1,0:T(8,128)(2,1)S(1)}, u32[]{:S(2)}, u32[]{:S(2)}) collective-permute-start(bf16[2,256,256]{2,1,0:T(8,128)(2,1)S(1)} %bitcast.63), channel_id=1, source_target_pairs={{0,1},{1,2},{2,3},{4,5},{5,6},{6,7},{8,9},{9,10},{10,11},{12,13},{... | collective-permute-start | bytes 786440 | tf_op jit(solution)/shard_map/ppermute | solution.py:835
  13.2 9.7 %collective-permute-start.1 = (bf16[2,256,256]{2,1,0:T(8,128)(2,1)S(1)}, bf16[2,256,256]{2,1,0:T(8,128)(2,1)S(1)}, u32[]{:S(2)}, u32[]{:S(2)}) collective-permute-start(bf16[2,256,256]{2,1,0:T(8,128)(2,1)S(1)} %bitcast.62), channel_id=1, source_target_pairs={{1,0},{2,1},{3,2},{5,4},{6,5},{7,6},{9,8},{10,9},{11,10},{13,12},{... | collective-permute-start | bytes 786440 | tf_op jit(solution)/shard_map/ppermute | solution.py:835
  37.4 9.8 %all-to-all-start = ((f32[4,32,256]{2,1,0:T(8,128)}), f32[4,32,256]{2,1,0:T(8,128)S(1)}, u32[]{:S(2)}, u32[]{:S(2)}) async-start(f32[4,32,256]{2,1,0:T(8,128)} %get-tuple-element.63), calls=%async_computation | async-start | bytes 262144 | tf_op jit(solution)/shard_map/all_to_all | solution.py:828
  62.8 16.8 %all-to-all-start.2 = ((f32[4,8,256]{2,1,0:T(8,128)}), f32[4,8,256]{2,1,0:T(8,128)S(1)}, u32[]{:S(2)}, u32[]{:S(2)}) async-start(f32[4,8,256]{2,1,0:T(8,128)} %get-tuple-element.70), calls=%async_computation.2 | async-start | bytes 65536 | tf_op jit(solution)/shard_map/all_to_all | solution.py:828
  79.6 18.1 %all-to-all-start.1 = ((f32[4,24,768]{2,1,0:T(8,128)}), f32[4,24,768]{2,1,0:T(8,128)S(1)}, u32[]{:S(2)}, u32[]{:S(2)}) async-start(f32[4,24,768]{2,1,0:T(8,128)} %get-tuple-element.67.refs_12_), calls=%async_computation.1 | async-start | bytes 589824 | tf_op jit(solution)/shard_map/all_to_all | solution.py:828
  97.7 12.2 %all-to-all-start.3 = ((f32[4,24,768]{2,1,0:T(8,128)}), f32[4,24,768]{2,1,0:T(8,128)S(1)}, u32[]{:S(2)}, u32[]{:S(2)}) async-start(f32[4,24,768]{2,1,0:T(8,128)} %get-tuple-element.71.refs_7_), calls=%async_computation.3 | async-start | bytes 589824 | tf_op jit(solution)/shard_map/all_to_all | solution.py:828
  109.9 9.8 %all-to-all-start.5 = ((bf16[4,32,768]{2,1,0:T(8,128)(2,1)}), bf16[4,32,768]{2,1,0:T(8,128)(2,1)S(1)}, u32[]{:S(2)}, u32[]{:S(2)}) async-start(bf16[4,32,768]{2,1,0:T(8,128)(2,1)} %get-tuple-element.73.refs_7_), calls=%async_computation.5 | async-start | bytes 393216 | tf_op jit(solution)/shard_map/all_to_all | solution.py:828
  119.6 13.9 %all-to-all-start.4 = ((bf16[4,32,768]{2,1,0:T(8,128)(2,1)}), bf16[4,32,768]{2,1,0:T(8,128)(2,1)S(1)}, u32[]{:S(2)}, u32[]{:S(2)}) async-start(bf16[4,32,768]{2,1,0:T(8,128)(2,1)} %get-tuple-element.76.refs_8_), calls=%async_computation.4 | async-start | bytes 393216 | tf_op jit(solution)/shard_map/all_to_all | solution.py:828
  133.6 19.2 %all-to-all-start.6 = ((bf16[8,256,256]{2,1,0:T(8,128)(2,1)}), bf16[8,256,256]{2,1,0:T(8,128)(2,1)S(1)}, u32[]{:S(2)}, u32[]{:S(2)}) async-start(bf16[8,256,256]{2,1,0:T(8,128)(2,1)} %bitcast.58), calls=%async_computation.6 | async-start | bytes 2097152 | tf_op jit(solution)/shard_map/all_to_all | solution.py:828
  152.7 18.9 %all-to-all-start.8 = ((bf16[8,256,256]{2,1,0:T(8,128)(2,1)}), bf16[8,256,256]{2,1,0:T(8,128)(2,1)S(1)}, u32[]{:S(2)}, u32[]{:S(2)}) async-start(bf16[8,256,256]{2,1,0:T(8,128)(2,1)} %bitcast.44), calls=%async_computation.8 | async-start | bytes 2097152 | tf_op jit(solution)/shard_map/all_to_all | solution.py:828
  171.6 14.6 %all-to-all-start.7 = ((f32[8,80,256]{2,1,0:T(8,128)}), f32[8,80,256]{2,1,0:T(8,128)S(1)}, u32[]{:S(2)}, u32[]{:S(2)}) async-start(f32[8,80,256]{2,1,0:T(8,128)} %bitcast.51), calls=%async_computation.7 | async-start | bytes 1310720 | tf_op jit(solution)/shard_map/all_to_all | solution.py:828
  186.3 18.9 %all-to-all-start.9 = ((bf16[8,256,256]{2,1,0:T(8,128)(2,1)}), bf16[8,256,256]{2,1,0:T(8,128)(2,1)S(1)}, u32[]{:S(2)}, u32[]{:S(2)}) async-start(bf16[8,256,256]{2,1,0:T(8,128)(2,1)} %add_parts.6.refs_1_.refs_2_), calls=%async_computation.9 | async-start | bytes 2097152 | tf_op jit(solution)/shard_map/all_to_all | solution.py:828
  189.8 11.1 %collective-permute-start.2 = (bf16[1,256,256]{2,1,0:T(8,128)(2,1)}, bf16[1,256,256]{2,1,0:T(8,128)(2,1)S(1)}, u32[]{:S(2)}, u32[]{:S(2)}) collective-permute-start(bf16[1,256,256]{2,1,0:T(8,128)(2,1)} %get-tuple-element.89), channel_id=1, source_target_pairs={{0,1},{1,2},{2,3},{4,5},{5,6},{6,7},{8,9},{9,10},{10,11},{12,13},{... | collective-permute-start | bytes 393224 | tf_op jit(solution)/shard_map/ppermute | solution.py:835
  193.8 7.6 %collective-permute-start.3 = (bf16[1,256,256]{2,1,0:T(8,128)(2,1)}, bf16[1,256,256]{2,1,0:T(8,128)(2,1)S(1)}, u32[]{:S(2)}, u32[]{:S(2)}) collective-permute-start(bf16[1,256,256]{2,1,0:T(8,128)(2,1)} %get-tuple-element.90), channel_id=1, source_target_pairs={{1,0},{2,1},{3,2},{5,4},{6,5},{7,6},{9,8},{10,9},{11,10},{13,12},{... | collective-permute-start | bytes 393224 | tf_op jit(solution)/shard_map/ppermute | solution.py:835
  210.3 22.4 %all-to-all-start.10 = ((bf16[8,256,256]{2,1,0:T(8,128)(2,1)}), bf16[8,256,256]{2,1,0:T(8,128)(2,1)S(1)}, u32[]{:S(2)}, u32[]{:S(2)}) async-start(bf16[8,256,256]{2,1,0:T(8,128)(2,1)} %hold.6), calls=%async_computation.10 | async-start | bytes 2097152 | tf_op jit(solution)/shard_map/all_to_all | solution.py:828
  214.0 39.5 %reduce-scatter.2.cloned.1.call-start = ((), (), s32[]{:S(2)}) async-start(), calls=%async_computation.16 | async-start | bytes 552960 | tf_op jit(solution)/shard_map/reduce_scatter | solution.py:1475
  214.0 11.4 %collective-permute-start.4 = (bf16[272,256]{1,0:T(8,128)(2,1)S(1)}, bf16[272,256]{1,0:T(8,128)(2,1)S(1)}, u32[]{:S(2)}, u32[]{:S(2)}) collective-permute-start(bf16[272,256]{1,0:T(8,128)(2,1)S(1)} %copy-done.37), channel_id=1, source_target_pairs={{0,1},{1,2},{2,3},{3,0},{4,5},{5,6},{6,7},{7,4},{8,9},{9,10},{10,1... | collective-permute-start | bytes 417800 | tf_op jit(solution)/shard_map/ppermute | solution.py:995
  216.1 9.3 %collective-permute-start.5 = (bf16[272,256]{1,0:T(8,128)(2,1)S(1)}, bf16[272,256]{1,0:T(8,128)(2,1)S(1)}, u32[]{:S(2)}, u32[]{:S(2)}) collective-permute-start(bf16[272,256]{1,0:T(8,128)(2,1)S(1)} %copy-done.36), channel_id=1, source_target_pairs={{0,3},{1,0},{2,1},{3,2},{4,7},{5,4},{6,5},{7,6},{8,11},{9,8},{10,9... | collective-permute-start | bytes 417800 | tf_op jit(solution)/shard_map/ppermute | solution.py:995
  218.2 7.2 %collective-permute-start.6 = (bf16[16,256]{1,0:T(8,128)(2,1)S(1)}, bf16[16,256]{1,0:T(8,128)(2,1)S(1)}, u32[]{:S(2)}, u32[]{:S(2)}) collective-permute-start(bf16[16,256]{1,0:T(8,128)(2,1)S(1)} %copy-done.25), channel_id=1, source_target_pairs={{0,2},{1,3},{2,0},{3,1},{4,6},{5,7},{6,4},{7,5},{8,10},{9,11},{10,... | collective-permute-start | bytes 24584 | tf_op jit(solution)/shard_map/ppermute | solution.py:995
  232.7 108.1 %all-gather.2.cloned.1.call-start = ((), (), s32[]{:S(2)}) async-start(), calls=%async_computation.17 | async-start | bytes 3649536 | tf_op jit(solution)/shard_map/all_gather | solution.py:1481
  253.5 27.8 %all-to-all-start.12 = ((f32[4,80,256]{2,1,0:T(8,128)}), f32[4,80,256]{2,1,0:T(8,128)S(1)}, u32[]{:S(2)}, u32[]{:S(2)}) async-start(f32[4,80,256]{2,1,0:T(8,128)} %add_parts.7.refs_2_), calls=%async_computation.12 | async-start | bytes 655360 | tf_op jit(solution)/shard_map/all_to_all | solution.py:828
  256.9 17.2 %collective-permute-start.7 = (bf16[272,256]{1,0:T(8,128)(2,1)}, bf16[272,256]{1,0:T(8,128)(2,1)S(1)}, u32[]{:S(2)}, u32[]{:S(2)}) collective-permute-start(bf16[272,256]{1,0:T(8,128)(2,1)} %get-tuple-element.97), channel_id=1, source_target_pairs={{0,1},{1,2},{2,3},{3,0},{4,5},{5,6},{6,7},{7,4},{8,9},{9,10},{10,1... | collective-permute-start | bytes 417800 | tf_op jit(solution)/shard_map/ppermute | solution.py:995
  258.9 15.3 %collective-permute-start.8 = (bf16[272,256]{1,0:T(8,128)(2,1)}, bf16[272,256]{1,0:T(8,128)(2,1)S(1)}, u32[]{:S(2)}, u32[]{:S(2)}) collective-permute-start(bf16[272,256]{1,0:T(8,128)(2,1)} %get-tuple-element.98), channel_id=1, source_target_pairs={{0,3},{1,0},{2,1},{3,2},{4,7},{5,4},{6,5},{7,6},{8,11},{9,8},{10,9... | collective-permute-start | bytes 417800 | tf_op jit(solution)/shard_map/ppermute | solution.py:995
  260.8 13.4 %collective-permute-start.9 = (bf16[16,256]{1,0:T(8,128)(2,1)}, bf16[16,256]{1,0:T(8,128)(2,1)S(1)}, u32[]{:S(2)}, u32[]{:S(2)}) collective-permute-start(bf16[16,256]{1,0:T(8,128)(2,1)} %get-tuple-element.96.refs_4_.refs_1_), channel_id=1, source_target_pairs={{0,2},{1,3},{2,0},{3,1},{4,6},{5,7},{6,4},{7,5},{8,10},{9,11},{10,... | collective-permute-start | bytes 24584 | tf_op jit(solution)/shard_map/ppermute | solution.py:995
  281.3 17.8 %all-to-all-start.11 = ((bf16[4,216,256]{2,1,0:T(8,128)(2,1)}), bf16[4,216,256]{2,1,0:T(8,128)(2,1)S(1)}, u32[]{:S(2)}, u32[]{:S(2)}) async-start(bf16[4,216,256]{2,1,0:T(8,128)(2,1)} %bitcast.57), calls=%async_computation.11 | async-start | bytes 884736 | tf_op jit(solution)/shard_map/all_to_all | solution.py:828
  301.7 22.5 %all-to-all-start.13 = ((bf16[4,216,256]{2,1,0:T(8,128)(2,1)}), bf16[4,216,256]{2,1,0:T(8,128)(2,1)S(1)}, u32[]{:S(2)}, u32[]{:S(2)}) async-start(bf16[4,216,256]{2,1,0:T(8,128)(2,1)} %add_parts.9.refs_3_), calls=%async_computation.13 | async-start | bytes 884736 | tf_op jit(solution)/shard_map/all_to_all | solution.py:828
  326.8 7.3 %collective-permute-start.10 = (bf16[27,32,128]{2,1,0:T(8,128)(2,1)}, bf16[27,32,128]{2,1,0:T(8,128)(2,1)S(1)}, u32[]{:S(2)}, u32[]{:S(2)}) collective-permute-start(bf16[27,32,128]{2,1,0:T(8,128)(2,1)} %bitcast.59), channel_id=1, source_target_pairs={{8,0},{12,4},{0,8},{4,12},{24,16},{28,20},{16,24},{20,28},{9,1},{1... | collective-permute-start | bytes 663560 | tf_op jit(solution)/shard_map/ppermute | solution.py:852
  328.3 7.0 %collective-permute-start.11 = (bf16[27,32,128]{2,1,0:T(8,128)(2,1)}, bf16[27,32,128]{2,1,0:T(8,128)(2,1)S(1)}, u32[]{:S(2)}, u32[]{:S(2)}) collective-permute-start(bf16[27,32,128]{2,1,0:T(8,128)(2,1)} %bitcast.64), channel_id=1, source_target_pairs={{16,0},{20,4},{24,8},{28,12},{0,16},{4,20},{8,24},{12,28},{17,1},{... | collective-permute-start | bytes 663560 | tf_op jit(solution)/shard_map/ppermute | solution.py:852
  338.3 10.9 %collective-permute-start.12 = (bf16[2,27,32,128]{3,2,1,0:T(8,128)(2,1)}, bf16[2,27,32,128]{3,2,1,0:T(8,128)(2,1)S(1)}, u32[]{:S(2)}, u32[]{:S(2)}) collective-permute-start(bf16[2,27,32,128]{3,2,1,0:T(8,128)(2,1)} %get-tuple-element.103.refs_0_), channel_id=1, source_target_pairs={{16,0},{20,4},{24,8},{28,12},{0,16},{4,20},{8,24},{12,28},{17,1},{... | collective-permute-start | bytes 1327112 | tf_op jit(solution)/shard_map/ppermute | solution.py:852
  339.8 10.6 %collective-permute-start.13 = (bf16[2,27,32,128]{3,2,1,0:T(8,128)(2,1)}, bf16[2,27,32,128]{3,2,1,0:T(8,128)(2,1)S(1)}, u32[]{:S(2)}, u32[]{:S(2)}) collective-permute-start(bf16[2,27,32,128]{3,2,1,0:T(8,128)(2,1)} %get-tuple-element.104.refs_2_), channel_id=1, source_target_pairs={{8,0},{12,4},{0,8},{4,12},{24,16},{28,20},{16,24},{20,28},{9,1},{1... | collective-permute-start | bytes 1327112 | tf_op jit(solution)/shard_map/ppermute | solution.py:852
  354.0 18.3 %collective-permute-start.14 = (bf16[2,4,27,32,128]{4,3,2,1,0:T(8,128)(2,1)}, bf16[2,4,27,32,128]{4,3,2,1,0:T(8,128)(2,1)S(1)}, u32[]{:S(2)}, u32[]{:S(2)}) collective-permute-start(bf16[2,4,27,32,128]{4,3,2,1,0:T(8,128)(2,1)} %bitcast.45), channel_id=1, source_target_pairs={{4,0},{0,4},{12,8},{8,12},{20,16},{16,20},{28,24},{24,28},{5,1},{1... | collective-permute-start | bytes 5308424 | tf_op jit(solution)/shard_map/ppermute | solution.py:852
  354.0 14.6 %all-to-all-start.14 = ((f32[8,80,256]{2,1,0:T(8,128)}), f32[8,80,256]{2,1,0:T(8,128)S(1)}, u32[]{:S(2)}, u32[]{:S(2)}) async-start(f32[8,80,256]{2,1,0:T(8,128)} %add_parts.8.refs_1_), calls=%async_computation.15 | async-start | bytes 1310720 | tf_op jit(solution)/shard_map/all_to_all | solution.py:828
  (38 other events, 161.4 us)
Sparse Core Ops, SparseCore 0:
  232.8 20.6 reduce-scatter.1
  256.6 68.1 all-gather.1
